TPU v7x, 128 devices: a whole 4x4x4 slice. The times are simulated.
128 devices in a mesh: dp: 16 (over y, x), feat: 8 (over z, core).
Axes of the slice: x: 4, y: 4, z: 4, core: 2. Of those that a mesh axis runs over, the one named last changes fastest.
Arguments:
- features: bfloat16 [8192, 8192], P('dp'), may hold values from -64 to 64
- proj_weight: bfloat16 [8192, 2048], P('dp', 'feat'), may hold values from -0.0625 to 0.0625
- partner: int32 [8192], P('dp'), may hold values from 0 to 8191, as said below
Outputs:
- grad_proj: float32 [8192, 2048], P('dp', 'feat')
Inputs may be any that keep to these rules, and one draw needn't show every extreme that they name: Pairing is mutual (partner[partner[i]] = i). The rows of each aligned block d of 512 rows are paired, in some order, with the rows of block (d + 8) mod (16).
All inputs are finite; a program needn't handle non-finite values.
Results may differ from a plain program's by a relative error of at most 0.03.
Values may be sent and summed in bfloat16 or wider, within the bound.
No kernel may reach another device: no remote copies, remote signals or barrier semaphores. Data moves between devices by JAX's collectives and lax.ppermute only.
A program may use at most 384 MiB of HBM per device.

v0:
```python
import math

import jax
import jax.numpy as jnp
from jax import lax
from jax.sharding import PartitionSpec as P

ridge = 0.0001
norm_eps = 1e-06


def from_behind(array, axis, by):
    peers = lax.axis_size(axis)
    return lax.ppermute(array, axis, [(i, (i + by) % peers) for i in range(peers)])


def build_pack(left_first, left_second, right_whole, owner_idx, blk_width):
    emb_width = right_whole.shape[1]
    highest = lax.Precision.HIGHEST
    first_rows = jnp.einsum(
        "ra,rc->ac", left_first, right_whole, preferred_element_type=jnp.float32, precision=highest
    )
    second_rows = jnp.einsum(
        "ra,rc->ac", left_second, right_whole, preferred_element_type=jnp.float32, precision=highest
    )
    joined = jnp.concatenate([first_rows, second_rows], axis=1)
    lead_cols = (owner_idx + 1) * blk_width
    shifted = lax.dynamic_slice_in_dim(joined, emb_width - lead_cols, emb_width + blk_width, 1)
    column = lax.broadcasted_iota(jnp.int32, (1, emb_width + blk_width), 1)
    return jnp.where(column < lead_cols, joined[:, : emb_width + blk_width], shifted)


def gather_packs(packed, feat_count):
    blk_width = packed.shape[0]
    pack_cols = packed.shape[1]
    summed = lax.psum(packed, "dp")
    stacked = lax.all_gather(summed, "feat", axis=0, tiled=True)
    return stacked.reshape(feat_count, blk_width, pack_cols)


def unpack_lower(stacked, feat_count, blk_width, emb_width):
    block_total = 2 * feat_count
    pieces = [None] * block_total
    for owner_idx in range(feat_count):
        lead_cols = (owner_idx + 1) * blk_width
        tail_cols = (block_total - owner_idx) * blk_width
        pieces[owner_idx] = jnp.pad(
            stacked[owner_idx, :, :lead_cols], ((0, 0), (0, emb_width - lead_cols))
        )
        pieces[block_total - 1 - owner_idx] = jnp.pad(
            stacked[owner_idx, :, lead_cols : lead_cols + tail_cols],
            ((0, 0), (0, emb_width - tail_cols)),
        )
    return jnp.concatenate(pieces, axis=0)


def body(features, proj_weight, partner):
    row_count = features.shape[0]
    feat_count = lax.axis_size("feat")
    dp_count = lax.axis_size("dp")
    own_cols = proj_weight.shape[1]
    emb_width = own_cols * feat_count
    block_total = 2 * feat_count
    blk_width = emb_width // block_total
    batch_size = row_count * dp_count
    feat_idx = lax.axis_index("feat")
    dp_idx = lax.axis_index("dp")
    second_blk = block_total - 1 - feat_idx
    highest = lax.Precision.HIGHEST
    slab_cols = features
    projected = jnp.dot(
        slab_cols,
        lax.all_gather(proj_weight, "dp", axis=0, tiled=True),
        preferred_element_type=jnp.float32,
    )
    col_mean = lax.psum(jnp.sum(projected, axis=0), "dp") / batch_size
    own_centered = (projected - col_mean).astype(jnp.bfloat16)
    centered = lax.all_gather(own_centered, "feat", axis=1, tiled=True)

    def pick_cols(matrix, blk_index):
        return lax.dynamic_slice_in_dim(matrix, blk_index * blk_width, blk_width, 1)

    def pick_rows(matrix, blk_index):
        return lax.dynamic_slice_in_dim(matrix, blk_index * blk_width, blk_width, 0)

    def own_blocks(matrix):
        return jnp.concatenate([pick_cols(matrix, feat_idx), pick_cols(matrix, second_blk)], axis=1)

    cov_pack = build_pack(
        pick_cols(centered, feat_idx),
        pick_cols(centered, second_blk),
        centered,
        feat_idx,
        blk_width,
    )
    cov_lower = unpack_lower(gather_packs(cov_pack, feat_count), feat_count, blk_width, emb_width)
    identity = jnp.eye(emb_width, dtype=jnp.float32)
    covariance = (jnp.tril(cov_lower) + jnp.tril(cov_lower, -1).T) / batch_size + ridge * identity
    factor = jnp.linalg.cholesky(covariance)
    whitener = lax.linalg.triangular_solve(factor, identity, left_side=True, lower=True)
    whitened = jnp.einsum("rc,ac->ra", centered.astype(jnp.float32), whitener, precision=highest)
    inv_norm = lax.rsqrt(jnp.sum(whitened * whitened, axis=1) + norm_eps)
    unit_rows = whitened * inv_norm[:, None]
    received = from_behind(whitened.astype(jnp.bfloat16), "dp", dp_count // 2).astype(
        whitened.dtype
    )
    local_pos = partner - (dp_idx + dp_count // 2) % dp_count * row_count
    mate_white = jnp.take(received, local_pos, axis=0)
    mate_inv = lax.rsqrt(jnp.sum(mate_white * mate_white, axis=1) + norm_eps)
    mate_rows = mate_white * mate_inv[:, None]
    pair_diff = unit_rows - mate_rows
    grad_unit = 4.0 / math.sqrt(batch_size) * pair_diff
    row_dots = jnp.sum(unit_rows * grad_unit, axis=1)
    grad_white = inv_norm[:, None] * (grad_unit - unit_rows * row_dots[:, None])
    grad_own = own_blocks(grad_white)
    mom_pack = build_pack(
        grad_own[:, :blk_width], grad_own[:, blk_width:], whitened, feat_idx, blk_width
    )
    mom_lower = unpack_lower(gather_packs(mom_pack, feat_count), feat_count, blk_width, emb_width)
    lower_part = jnp.tril(mom_lower, -1) + 0.5 * jnp.diag(jnp.diag(mom_lower))
    sym = lower_part + lower_part.T
    own_sym = own_blocks(sym)
    back_white = grad_own - jnp.dot(whitened, own_sym, precision=highest) / batch_size
    own_whiten = jnp.concatenate(
        [pick_rows(whitener, feat_idx), pick_rows(whitener, second_blk)], axis=0
    )
    back_term = jnp.dot(back_white, own_whiten, precision=highest)
    back_center = lax.psum_scatter(back_term, "feat", scatter_dimension=1, tiled=True)
    back_mean = lax.psum(jnp.sum(back_center, axis=0), "dp") / batch_size
    back_proj = (back_center - back_mean).astype(jnp.bfloat16)
    slab_cols = features
    return lax.psum_scatter(
        jnp.einsum("rf,rc->fc", slab_cols, back_proj, preferred_element_type=jnp.float32).astype(
            jnp.bfloat16
        ),
        "dp",
        scatter_dimension=0,
        tiled=True,
    ).astype(jnp.float32)


def solution(mesh):
    return jax.shard_map(
        body,
        mesh=mesh,
        in_specs=(P("dp", None), P("dp", "feat"), P("dp")),
        out_specs=P("dp", "feat"),
        check_vma=False,
    )
```

profile of v0, /device:TPU:0, one launch (start us, length us, event | category | flops | bytes accessed | tf_op | source)
XLA Modules:
  0.0 1903.4 jit_solution(5074336157813921863)
XLA Ops:
  7.3 56.1 %all-gather.5.cloned.1.call-done = bf16[8192,256]{1,0:T(8,128)(2,1)} async-done(((bf16[512,256]{1,0:T(8,128)(2,1)}), bf16[8192,256]{1,0:T(8,128)(2,1)}) %all-gather.5.cloned.1.call-update) | async-done | bytes 4194320 | tf_op jit(solution)/shard_map/all_gather | solution.py:73
  70.3 38.4 %psum.28 = f32[256]{0:T(256)S(1)} all-reduce(f32[256]{0:T(256)S(1)} %get-tuple-element.196), channel_id=1, replica_groups=mesh['dp'=16,'feat'=8] {'dp'}, use_global_device_ids=true, to_apply=%region_1.0 | all-reduce | flops 256 | bytes 2048 | tf_op jit(solution)/shard_map/psum | solution.py:76
  109.6 23.9 %all-gather.7.cloned.1.call-done = bf16[512,2048]{1,0:T(8,128)(2,1)} async-done(((bf16[512,256]{1,0:T(8,128)(2,1)}), bf16[512,2048]{1,0:T(8,128)(2,1)}) %all-gather.7.cloned.1.call-update) | async-done | bytes 2097168 | tf_op jit(solution)/shard_map/all_gather | solution.py:78
  139.2 87.6 %all-reduce.34.cloned.1.call-done = f32[128,2176]{1,0:T(8,128)} async-done(((f32[128,2176]{1,0:T(8,128)}), f32[128,2176]{1,0:T(8,128)}) %all-reduce.34.cloned.1.call-update) | async-done | bytes 1114128 | tf_op jit(solution)/shard_map/psum | solution.py:36
  238.8 41.0 %all-gather.9.cloned.1.call-done = f32[1024,2176]{1,0:T(8,128)} async-done(((f32[128,2176]{1,0:T(8,128)}), f32[1024,2176]{1,0:T(8,128)}) %all-gather.9.cloned.1.call-update) | async-done | bytes 8912912 | tf_op jit(solution)/shard_map/all_gather | solution.py:37
  359.3 12.4 fusion.3
  371.7 17.6 copy.63
  389.3 17.3 fusion.2
  406.6 17.6 copy.64
  424.2 11.9 fusion
  441.8 11.7 cholesky.456
  453.6 9.8 custom-call.126
  467.7 11.7 cholesky.479
  479.9 10.2 custom-call.127
  503.4 11.7 cholesky.502
  515.9 9.9 custom-call.128
  534.1 11.7 cholesky.523
  546.6 10.0 custom-call.129
  565.6 11.7 cholesky.960
  578.1 10.2 custom-call.130
  598.2 11.7 cholesky.980
  610.7 9.9 custom-call.131
  630.9 11.7 cholesky.1000
  643.4 10.0 custom-call.132
  655.0 9.1 fusion.42
  664.1 12.1 cholesky.1020
  677.0 9.8 custom-call.133
  688.2 9.1 fusion.77
  697.3 11.9 cholesky.1040
  710.0 9.8 custom-call.134
  721.2 9.1 fusion.86
  730.3 11.9 cholesky.1060
  743.0 9.8 custom-call.135
  762.8 12.1 cholesky.1080
  775.7 9.8 custom-call.136
  794.8 11.9 cholesky.1100
  807.4 9.8 custom-call.137
  825.6 11.9 cholesky.1120
  838.3 9.8 custom-call.138
  855.4 12.1 cholesky.1140
  868.3 9.8 custom-call.139
  883.9 11.7 cholesky.1160
  896.4 9.8 custom-call.140
  910.7 11.7 cholesky.1178
  943.4 12.5 select_select_fusion
  955.8 59.7 %while.1 = (s32[]{:T(128)}, f32[2048,2048]{0,1:T(8,128)}, s32[16,2]{0,1:T(2,128)S(1)}, f32[16,128,128]{2,1,0:T(8,128)}, s32[]{:T(128)}) while((s32[]{:T(128)}, f32[2048,2048]{0,1:T(8,128)}, s32[16,2]{0,1:T(2,128)S(1)}, f32[16,128,128]{2,1,0:T(8,128)}, s32[]{:T(128)}) %tuple.158), condition=%wide.while_cond, body=%wide.while_body.sunk | while | flops 2 | bytes 393829 | solution.py:100
  1015.5 158.8 %custom-call.141 = f32[16,128,128]{1,2,0:T(8,128)} custom-call(f32[16,128,128]{2,1,0:T(8,128)} %get-tuple-element.12), custom_call_target="InvertDiagBlocksLowerTriangular" | custom-call | tf_op jit(solution)/shard_map/triangular_solve | solution.py:100
  1294.8 9.0 convolution_subtract_fusion.2
  1320.2 10.2 convolution_subtract_fusion.11
  1334.4 10.9 convolution_subtract_fusion.14
  1349.1 11.7 convolution_subtract_fusion.12
  1364.3 12.3 convolution_subtract_fusion.13
  1379.5 19.3 %multiply_reduce_fusion.2 = (f32[512]{0:T(512)S(1)}, bf16[512,2048]{1,0:T(8,128)(2,1)}, f32[512,2048]{1,0:T(8,128)}) fusion(bf16[512,2048]{1,0:T(8,128)(2,1)S(1)} %copy-done.7, f32[2048,2048]{1,0:T(8,128)} %convolution_dynamic-update-slice_fusion.3), kind=kOutput, calls=%fused_computation.33 | convolution fusion | flops 25772949504 | bytes 25167872 | tf_op jit(solution)/shard_map/rc,ac->ra/dot_general | solution.py:101
  1401.8 46.5 %collective-permute-done = bf16[512,2048]{1,0:T(8,128)(2,1)S(1)} collective-permute-done((bf16[512,2048]{1,0:T(8,128)(2,1)}, bf16[512,2048]{1,0:T(8,128)(2,1)S(1)}, u32[]{:S(2)}, u32[]{:S(2)}) %collective-permute-start) | collective-permute-done | bytes 2097184 | tf_op jit(solution)/shard_map/ppermute | solution.py:14
  1474.1 86.8 %all-reduce.36.cloned.1.call-done = f32[128,2176]{1,0:T(8,128)} async-done(((f32[128,2176]{1,0:T(8,128)}), f32[128,2176]{1,0:T(8,128)}) %all-reduce.36.cloned.1.call-update) | async-done | bytes 1114128 | tf_op jit(solution)/shard_map/psum | solution.py:36
  1566.7 11.3 copy.99
  1579.6 34.2 %all-gather.11.cloned.1.call-done = f32[1024,2176]{1,0:T(8,128)} async-done(((f32[128,2176]{1,0:T(8,128)}), f32[1024,2176]{1,0:T(8,128)}) %all-gather.11.cloned.1.call-update) | async-done | bytes 8912912 | tf_op jit(solution)/shard_map/all_gather | solution.py:37
  1648.9 34.1 %gather_fusion.1 = f32[2048]{0:T(1024)S(1)} fusion(f32[2048,2048]{1,0:T(8,128)} %fusion.110, s32[2048]{0:T(1024)S(1)} %bitcast.272), kind=kCustom, calls=%fused_computation.1 | custom fusion | bytes 32768 | tf_op jit(solution)/shard_map/jit(_diag)/jit(diagonal)/cond/branch_0_fun/gather | solution.py:120
  1682.9 14.3 multiply_add_fusion
  1697.2 17.6 copy.100
  1714.8 11.8 bitcast_add_fusion
  1735.6 38.4 %reduce-scatter.3.cloned.1.call-done = f32[512,256]{1,0:T(8,128)} async-done(((f32[512,2048]{1,0:T(8,128)}), f32[512,256]{1,0:T(8,128)}) %reduce-scatter.3.cloned.1.call-update) | async-done | bytes 524304 | tf_op jit(solution)/shard_map/reduce_scatter | solution.py:128
  1775.0 40.5 %psum.31 = f32[256]{0:T(256)S(1)} all-reduce(f32[256]{0:T(256)S(1)} %reduce_sum.49), channel_id=1, replica_groups=mesh['dp'=16,'feat'=8] {'dp'}, use_global_device_ids=true, to_apply=%region_41.42 | all-reduce | flops 256 | bytes 2048 | tf_op jit(solution)/shard_map/psum | solution.py:129
  1823.5 71.0 %reduce-scatter.5.cloned.1.call-done = bf16[512,256]{0,1:T(8,128)(2,1)} async-done(((bf16[8192,256]{0,1:T(8,128)(2,1)}), bf16[512,256]{0,1:T(8,128)(2,1)}) %reduce-scatter.5.cloned.1.call-update) | async-done | bytes 262160 | tf_op jit(solution)/shard_map/reduce_scatter | solution.py:132
  (388 shorter events, 538.5 us)
Async XLA Ops:
  6.5 56.9 %all-gather.5.cloned.1.call-start = ((), (), s32[]{:S(2)}) async-start(), calls=%async_computation.2 | async-start | bytes 4456448 | tf_op jit(solution)/shard_map/all_gather | solution.py:73
  7.3 126.3 %all-gather.7.cloned.1.call-start = ((), (), s32[]{:S(2)}) async-start(), calls=%async_computation.3 | async-start | bytes 2359296 | tf_op jit(solution)/shard_map/all_gather | solution.py:78
  109.5 117.3 %all-reduce.34.cloned.1.call-start = ((), (), s32[]{:S(2)}) async-start(), calls=%async_computation.4 | async-start | bytes 2228224 | tf_op jit(solution)/shard_map/psum | solution.py:36
  109.6 129.2 %copy-start.14 = (pred[2176]{0:T(1024)(128)(4,1)}, pred[2176]{0:T(1024)(128)(4,1)S(1)}, u32[]{:S(2)}) copy-start(pred[2176]{0:T(1024)(128)(4,1)S(1)} %iota_compare_fusion.5) | copy-start | bytes 6532
  139.1 140.7 %all-gather.9.cloned.1.call-start = ((), (), s32[]{:S(2)}) async-start(), calls=%async_computation.5 | async-start | bytes 10027008 | tf_op jit(solution)/shard_map/all_gather | solution.py:37
  226.8 1334.1 %all-reduce.36.cloned.1.call-start = ((), (), s32[]{:S(2)}) async-start(), calls=%async_computation.6 | async-start | bytes 2228224 | tf_op jit(solution)/shard_map/psum | solution.py:36
  227.1 162.2 %copy-start.12 = (s32[2048]{0:T(1024)}, s32[2048]{0:T(1024)S(1)}, u32[]{:S(2)}) copy-start(s32[2048]{0:T(1024)S(1)} %iota_add_fusion) | copy-start | bytes 24580
  320.4 23.6 %copy-start.11 = (f32[1,128,896]{1,2,0:T(8,128)S(1)}, f32[1,128,896]{1,2,0:T(8,128)}, u32[]{:S(2)}) copy-start(f32[1,128,896]{1,2,0:T(8,128)} %copy.123) | copy-start | bytes 1376260
  333.6 20.2 %copy-start.10 = (f32[1,128,1536]{1,2,0:T(8,128)S(1)}, f32[1,128,1536]{1,2,0:T(8,128)}, u32[]{:S(2)}) copy-start(f32[1,128,1536]{1,2,0:T(8,128)} %copy.128) | copy-start | bytes 2359300
  333.6 21.3 %copy-start.9 = (f32[1,128,1664]{1,2,0:T(8,128)S(1)}, f32[1,128,1664]{1,2,0:T(8,128)}, u32[]{:S(2)}) copy-start(f32[1,128,1664]{1,2,0:T(8,128)} %copy.129) | copy-start | bytes 2555908
  333.6 22.4 %copy-start.8 = (f32[1,128,1792]{1,2,0:T(8,128)S(1)}, f32[1,128,1792]{1,2,0:T(8,128)}, u32[]{:S(2)}) copy-start(f32[1,128,1792]{1,2,0:T(8,128)} %copy.130) | copy-start | bytes 2752516
  436.1 5.7 copy-start.4
  493.4 5.7 copy-start
  1174.4 17.7 slice-start
  1174.4 17.7 slice-start.1
  1181.1 10.9 slice-start.2
  1184.6 7.5 slice-start.3
  1192.0 23.2 %copy-start.6 = (f32[128,2048]{1,0:T(8,128)}, f32[128,2048]{1,0:T(8,128)S(1)}, u32[]{:S(2)}) copy-start(f32[128,2048]{1,0:T(8,128)S(1)} %get-tuple-element.199) | copy-start | bytes 3145732
  1265.5 3.6 copy-start.5
  1360.8 18.7 copy-start.7
  1379.5 22.3 %copy-start.16 = (s32[512]{0:T(512)S(1)}, s32[512]{0:T(512)}, u32[]{:S(2)}) copy-start(s32[512]{0:T(512)} %param.5) | copy-start | bytes 6148
  1398.7 49.5 %collective-permute-start = (bf16[512,2048]{1,0:T(8,128)(2,1)}, bf16[512,2048]{1,0:T(8,128)(2,1)S(1)}, u32[]{:S(2)}, u32[]{:S(2)}) collective-permute-start(bf16[512,2048]{1,0:T(8,128)(2,1)} %get-tuple-element.40), channel_id=1, source_target_pairs={{0,64},{8,72},{16,80},{24,88},{32,96},{40,104},{48,112},{56,120},{... | collective-permute-start | bytes 6291464 | tf_op jit(solution)/shard_map/ppermute | solution.py:14
  1458.5 7.8 copy-start.1
  1458.5 7.8 copy-start.3
  1461.4 11.3 copy-start.15
  1466.3 94.6 %copy-start.13 = (s32[2048]{0:T(1024)S(1)}, s32[2048]{0:T(1024)}, u32[]{:S(2)}) copy-start(s32[2048]{0:T(1024)} %copy-done.12) | copy-start | bytes 24580
  1474.0 139.8 %all-gather.11.cloned.1.call-start = ((), (), s32[]{:S(2)}) async-start(), calls=%async_computation.7 | async-start | bytes 10027008 | tf_op jit(solution)/shard_map/all_gather | solution.py:37
  1560.9 213.0 %reduce-scatter.3.cloned.1.call-start = ((), (), s32[]{:S(2)}) async-start(), calls=%async_computation.8 | async-start | bytes 4718592 | tf_op jit(solution)/shard_map/reduce_scatter | solution.py:128
  1714.8 12.1 copy-start.2
  1735.5 158.9 %reduce-scatter.5.cloned.1.call-start = ((), (), s32[]{:S(2)}) async-start(), calls=%async_computation.9 | async-start | bytes 4456448 | tf_op jit(solution)/shard_map/reduce_scatter | solution.py:132
Sparse Core Ops, SparseCore 0:
  9.5 53.8 all-gather.4
  109.6 23.8 all-gather.6
  139.3 87.4 all-reduce.33
  228.4 51.3 all-gather.8
  1474.1 86.7 all-reduce.35
  1562.4 51.3 all-gather.10
  1735.6 38.2 reduce-scatter.2
  1823.6 70.8 reduce-scatter.4
where the time goes:
time: 1910 us; the launch traced here: 1900 us
  other arithmetic  621 us (33%)
  waiting for transfers between devices  486 us (25%)
  matrix products  377 us (20%)
  local copies, waits for them, and re-layouts  312 us (16%)
  blocking collectives  79 us (4%)
  between operations  24.9 us (1%)
    another operation x62, other arithmetic, body(): factor = jnp.linalg.cholesky(covariance)  348 us
    another operation x31, matrix products, body(): lax.linalg.triangular_solve(factor, identity, left_side=True, lower=True)  201 us
    psum x2, waiting for transfers between devices, gather_packs(): summed = lax.psum(packed, 'dp')  174 us
    another operation x3, other arithmetic, body(): lax.linalg.triangular_solve(factor, identity, left_side=True, lower=True)  171 us
    another operation x30, matrix products, body(): factor = jnp.linalg.cholesky(covariance)  124 us
    unnamed x88, local copies, waits for them, and re-layouts  83.4 us
    all_gather x2, waiting for transfers between devices, gather_packs(): stacked = lax.all_gather(summed, 'feat', axis=0, tiled=True)  75.2 us
    reduce_scatter x1, waiting for transfers between devices, body(): lax.psum_scatter(jnp.einsum('rf,rc->fc', slab_cols, back_proj, preferred_...  71 us
  transfers between devices with their start and end apart: 9, of which 9 were waited for; matrix products, arithmetic and copies ran while one was open for 2% of the time, Pallas kernels for 0%

commit v1 on v0

v1 whole, which is shorter than its diff:
```python
import math

import jax
import jax.numpy as jnp
from jax import lax
from jax.experimental import pallas as pl
from jax.experimental.pallas import tpu as pltpu
from jax.sharding import PartitionSpec as P

ridge = 0.0001
norm_eps = 1e-06
f32 = jnp.float32
bf16 = jnp.bfloat16


def from_behind(array, axis, by):
    peers = lax.axis_size(axis)
    return lax.ppermute(array, axis, [(i, (i + by) % peers) for i in range(peers)])


def split_two(value):
    high = value.astype(bf16)
    return high, (value - high.astype(f32)).astype(bf16)


def mat(left, right):
    return jnp.dot(left, right, preferred_element_type=f32)


def mat_high(left, right):
    return jnp.dot(left, right, preferred_element_type=f32, precision=lax.Precision.HIGHEST)


def invert_small(matrix):
    size = matrix.shape[0]
    groups = size // 8
    lane = lax.broadcasted_iota(jnp.int32, (8, size), 1)
    sub = lax.broadcasted_iota(jnp.int32, (8, size), 0)
    rows = [matrix[8 * i : 8 * i + 8] for i in range(groups)]
    for g in range(groups):
        base = 8 * g
        panel = rows[g]
        inside = (lane >= base) & (lane < base + 8)
        cols = [
            jnp.broadcast_to(panel[:, base + j : base + j + 1], (8, size)) for j in range(8)
        ]
        panel = jnp.where(inside, jnp.where(lane - base == sub, 1.0, 0.0), panel)
        for j in range(8):
            inv = 1.0 / jnp.broadcast_to(cols[j][j : j + 1, :], (8, size))
            here = sub == j
            factor = cols[j] * inv
            pivot_row = jnp.broadcast_to(panel[j : j + 1, :], (8, size))
            for m in range(j + 1, 8):
                entry = jnp.broadcast_to(cols[m][j : j + 1, :], (8, size))
                cols[m] = jnp.where(here, entry * inv, cols[m] - factor * entry)
            panel = jnp.where(here, pivot_row * inv, panel - factor * pivot_row)
        spread = [jnp.broadcast_to(panel[j : j + 1, :], (8, size)) for j in range(8)]
        for i in list(range(g + 1, groups)) + list(range(g)):
            old = rows[i]
            total = jnp.where(inside, 0.0, old)
            for j in range(8):
                total = total - (
                    jnp.broadcast_to(old[:, base + j : base + j + 1], (8, size)) * spread[j]
                )
            rows[i] = total
        rows[g] = panel
    return jnp.concatenate(rows, axis=0)


def invert_panel(block):
    half = block.shape[0] // 2
    b11, b12 = block[:half, :half], block[:half, half:]
    b21, b22 = block[half:, :half], block[half:, half:]
    p1 = invert_small(b11)
    r1 = mat_high(p1, b12)
    low = mat_high(b21, p1)
    p2 = invert_small(b22 - mat_high(b21, r1))
    q = mat_high(r1, p2)
    top = jnp.concatenate([p1 + mat_high(q, low), -q], axis=1)
    bottom = jnp.concatenate([-mat_high(p2, low), p2], axis=1)
    return jnp.concatenate([top, bottom], axis=0)


def inverse_kernel(batch_size, packed, out, work, left, right, fresh):
    pairs, blk, _ = packed.shape
    blocks = 2 * pairs
    size = work.shape[0]
    wide = fresh.shape[0]
    steps = size // wide
    diagonal = lax.broadcasted_iota(jnp.int32, (blk, blk), 0) == lax.broadcasted_iota(
        jnp.int32, (blk, blk), 1
    )
    ridge_tile = jnp.where(diagonal, ridge, 0.0)
    for a in range(blocks):
        for c in range(a + 1):
            if a < pairs:
                tile = packed[a, :, c * blk : (c + 1) * blk]
            else:
                at = (blocks - a + c) * blk
                tile = packed[blocks - 1 - a, :, at : at + blk]
            tile = tile * (1.0 / batch_size)
            if c == a:
                tile = tile + ridge_tile
            work[a * blk : (a + 1) * blk, c * blk : (c + 1) * blk] = tile
            if c != a:
                work[c * blk : (c + 1) * blk, a * blk : (a + 1) * blk] = tile.T

    def step(k, carry):
        at_k = pl.ds(pl.multiple_of(k * wide, wide), wide)
        pivot = invert_panel(work[at_k, at_k])
        pivot_high, pivot_low = split_two(pivot)
        for i in range(steps):
            rows = slice(i * wide, (i + 1) * wide)
            high, low = split_two(work[rows, at_k])
            left[rows, :wide] = high
            left[rows, wide : 2 * wide] = low
            left[rows, 2 * wide :] = high
        for j in range(steps):
            lanes = slice(j * wide, (j + 1) * wide)
            high, low = split_two(work[at_k, lanes])
            fresh[:, lanes] = mat(pivot_high, high) + (
                mat(pivot_high, low) + mat(pivot_low, high)
            )
        fresh[:, at_k] = pivot
        for j in range(steps):
            lanes = slice(j * wide, (j + 1) * wide)
            high, low = split_two(fresh[:, lanes])
            right[:wide, lanes] = high
            right[wide : 2 * wide, lanes] = high
            right[2 * wide :, lanes] = low
        work[:, at_k] = jnp.zeros((size, wide), f32)

        def update(j, inner):
            lanes = pl.ds(pl.multiple_of(j * wide, wide), wide)
            for part in range(2):
                rows = slice(part * size // 2, (part + 1) * size // 2)
                work[rows, lanes] = work[rows, lanes] - mat(left[rows, :], right[:, lanes])
            return inner

        lax.fori_loop(0, steps, update, 0)
        work[at_k, :] = fresh[...]
        return carry

    lax.fori_loop(0, steps, step, 0)
    for i in range(steps):
        rows = slice(i * wide, (i + 1) * wide)
        high, low = split_two(work[rows, :])
        out[0, rows, :] = high
        out[1, rows, :] = low


def inverse_parts(packed, size, batch_size, wide=256):
    return pl.pallas_call(
        lambda *refs: inverse_kernel(batch_size, *refs),
        out_shape=jax.ShapeDtypeStruct((2, size, size), bf16),
        scratch_shapes=[
            pltpu.VMEM((size, size), f32),
            pltpu.VMEM((size, 3 * wide), bf16),
            pltpu.VMEM((3 * wide, size), bf16),
            pltpu.VMEM((wide, size), f32),
        ],
        compiler_params=pltpu.CompilerParams(vmem_limit_bytes=60 * 2**20),
    )(packed)


def sum_shares(array, axis):
    return jnp.sum(
        lax.all_to_all(array, axis, 0, 0, tiled=True).astype(f32), axis=0
    )


def three_parts(vector):
    high = lax.reduce_precision(vector, 8, 7)
    rest = vector - high
    mid = lax.reduce_precision(rest, 8, 7)
    rows = jnp.stack([high, mid, rest - mid]).astype(bf16)
    return jnp.pad(rows, ((0, 13), (0, 0)))


def body(features, proj_weight, partner):
    row_count = features.shape[0]
    feat_count = lax.axis_size("feat")
    dp_count = lax.axis_size("dp")
    own_cols = proj_weight.shape[1]
    emb_width = own_cols * feat_count
    blk_width = emb_width // (2 * feat_count)
    batch_size = row_count * dp_count
    feat_idx = lax.axis_index("feat")
    dp_idx = lax.axis_index("dp")

    def own(matrix, axis=1):
        return lax.dynamic_slice_in_dim(matrix, feat_idx * own_cols, own_cols, axis)

    def pick_cols(matrix, blk_index):
        return lax.dynamic_slice_in_dim(matrix, blk_index * blk_width, blk_width, 1)

    weight = lax.all_gather(proj_weight, "dp", axis=0, tiled=True)
    feature_sum = jnp.sum(features.astype(f32), axis=0)
    feature_sum = jnp.sum(lax.all_gather(feature_sum, "dp"), axis=0)
    col_mean = jnp.sum(mat(three_parts(feature_sum), weight), axis=0) / batch_size
    own_centered = (mat(features, weight) - col_mean).astype(bf16)
    centered = lax.all_gather(own_centered, "feat", axis=1, tiled=True)

    received = from_behind(centered, "dp", dp_count // 2)
    first = mat(pick_cols(centered, feat_idx).T, centered)
    second = mat(pick_cols(centered, 2 * feat_count - 1 - feat_idx).T, centered)
    joined = jnp.concatenate([first, second], axis=1)
    lead_cols = (feat_idx + 1) * blk_width
    shifted = lax.dynamic_slice_in_dim(joined, emb_width - lead_cols, emb_width + blk_width, 1)
    column = lax.broadcasted_iota(jnp.int32, (1, emb_width + blk_width), 1)
    cov_pack = jnp.where(column < lead_cols, joined[:, : emb_width + blk_width], shifted)
    cov_share = sum_shares(
        cov_pack.reshape(dp_count, blk_width // dp_count, emb_width + blk_width), "dp"
    )
    packed = lax.all_gather(cov_share, ("feat", "dp"), axis=0, tiled=True)
    packed = packed.reshape(feat_count, blk_width, emb_width + blk_width)

    local_pos = partner - (dp_idx + dp_count // 2) % dp_count * row_count
    mates = jnp.take(received, local_pos, axis=0)
    center_sum = jnp.sum(centered.astype(f32), axis=0)
    center_sum = jnp.sum(lax.all_gather(center_sum, "dp"), axis=0)
    sum_rows = three_parts(center_sum)
    packed, mates, sum_rows = lax.optimization_barrier((packed, mates, sum_rows))

    parts = inverse_parts(packed, emb_width, batch_size)
    white_rows = mat(centered, parts[0]) + mat(centered, parts[1])
    mate_white = mat(mates, parts[0]) + mat(mates, parts[1])
    sum_white = jnp.sum(mat(sum_rows, parts[0]) + mat(sum_rows, parts[1]), axis=0)
    mates_wide = mates.astype(f32)
    norm_sq = jnp.sum(white_rows * centered.astype(f32), axis=1)
    cross = jnp.sum(white_rows * mates_wide, axis=1)
    mate_sq = jnp.sum(mate_white * mates_wide, axis=1)
    inv_norm = lax.rsqrt(norm_sq + norm_eps)
    mate_inv = lax.rsqrt(mate_sq + norm_eps)
    scale = 4.0 / math.sqrt(batch_size)
    alpha = scale * inv_norm * inv_norm * (
        cross * inv_norm * mate_inv + norm_eps * inv_norm * inv_norm
    )
    beta = -scale * inv_norm * mate_inv
    own_back = alpha[:, None] * own(white_rows) + beta[:, None] * own(mate_white)
    own_sum = jnp.sum(own_back, axis=0)

    moment = mat(centered.T, own_back.astype(bf16)) / batch_size
    shares = moment.reshape(dp_count, emb_width // dp_count, own_cols).astype(bf16)
    sum_high = lax.reduce_precision(own_sum, 8, 7)
    sum_two = jnp.stack([sum_high, own_sum - sum_high]).astype(bf16)
    sum_two = jnp.broadcast_to(jnp.pad(sum_two, ((0, 14), (0, 0))), (dp_count, 16, own_cols))
    reduced = sum_shares(jnp.concatenate([shares, sum_two], axis=1), "dp")
    own_total = reduced[-16] + reduced[-15]
    moment_share = reduced[:-16].astype(bf16)
    moment = lax.all_to_all(
        jnp.broadcast_to(moment_share, (dp_count,) + moment_share.shape), "dp", 0, 0, tiled=True
    ).reshape(emb_width, own_cols)
    back_center = own_back - mat(white_rows.astype(bf16), moment)
    sum_moment = jnp.sum(sum_white[:, None] * moment.astype(f32), axis=0)
    back_mean = (own_total - sum_moment) / batch_size
    back_proj = (back_center - back_mean).astype(bf16)
    grad = mat(features.T, back_proj).astype(bf16)
    return sum_shares(grad.reshape(dp_count, -1, own_cols), "dp")


def solution(mesh):
    return jax.shard_map(
        body,
        mesh=mesh,
        in_specs=(P("dp", None), P("dp", "feat"), P("dp")),
        out_specs=P("dp", "feat"),
        check_vma=False,
    )
```

time: 1910 us -> 550 us (0.29)
  other arithmetic: 621 us -> 14.5 us
  waiting for transfers between devices: 486 us -> 81.3 us
  matrix products: 377 us -> 62.2 us
  local copies, waits for them, and re-layouts: 312 us -> 10.3 us
  Pallas kernels: 0 us -> 167 us
  blocking collectives: 79 us -> 187 us
    another operation x65 -> x5, other arithmetic: 520 us -> 0.15 us  [the longest x62 348 us: body(): factor = jnp.linalg.cholesky(covariance)]
    another operation x61 -> x0, matrix products: 325 us -> none  [the longest x31 201 us: body(): lax.linalg.triangular_solve(factor, identity, left_side=True, lower=True)]
    psum x2 -> x0, waiting for transfers between devices: 174 us -> none  [gather_packs(): summed = lax.psum(packed, 'dp')]
    pallas_call x0 -> x1, Pallas kernels: none -> 167 us  [inverse_parts(): pl.pallas_call(lambda *refs: inverse_kernel(batch_size, *refs), out_shape...]
    reduce_scatter x2 -> x0, waiting for transfers between devices: 109 us -> none  [the longest x1 71 us: body(): lax.psum_scatter(jnp.einsum('rf,rc->fc', slab_cols, back_proj, preferred_...]
    all_to_all x0 -> x3, blocking collectives: none -> 101 us  [sum_shares(): lax.all_to_all(array, axis, 0, 0, tiled=True).astype(f32)]
    all_gather x0 -> x2, blocking collectives: none -> 85.9 us  [the longest x1 60.9 us: body(): center_sum = jnp.sum(lax.all_gather(center_sum, 'dp'), axis=0)]
    all_gather x3 -> x2, waiting for transfers between devices: 131 us -> 45.3 us  [the longest x1 26.1 us: body(): weight = lax.all_gather(proj_weight, 'dp', axis=0, tiled=True)]
  transfers between devices with their start and end apart: 9 -> 5, of which waited for: 9 -> 4; matrix products, arithmetic and copies ran while one was open for 2% -> 4% of each run, Pallas kernels for 0% -> 0%
where the time goes in v1:
time: 550 us; the launch traced here: 541 us
  blocking collectives  187 us (34%)
  Pallas kernels  167 us (30%)
  waiting for transfers between devices  81.3 us (15%)
  matrix products  62.2 us (11%)
  other arithmetic  14.5 us (3%)
  between operations  13.8 us (3%)
  local copies, waits for them, and re-layouts  10.3 us (2%)
    pallas_call x1, Pallas kernels, inverse_parts(): pl.pallas_call(lambda *refs: inverse_kernel(batch_size, *refs), out_shape...  167 us
    all_to_all x3, blocking collectives, sum_shares(): lax.all_to_all(array, axis, 0, 0, tiled=True).astype(f32)  101 us
    dot_general x12, matrix products, mat(): return jnp.dot(left, right, preferred_element_type=f32)  62.2 us
    all_gather x1, blocking collectives, body(): center_sum = jnp.sum(lax.all_gather(center_sum, 'dp'), axis=0)  60.9 us
    all_gather x1, waiting for transfers between devices, body(): centered = lax.all_gather(own_centered, 'feat', axis=1, tiled=True)  27.3 us
    all_gather x1, waiting for transfers between devices, body(): weight = lax.all_gather(proj_weight, 'dp', axis=0, tiled=True)  26.1 us
    all_gather x1, blocking collectives, body(): feature_sum = jnp.sum(lax.all_gather(feature_sum, 'dp'), axis=0)  25.1 us
    all_gather x1, waiting for transfers between devices, body(): packed = lax.all_gather(cov_share, ('feat', 'dp'), axis=0, tiled=True)  19.3 us
  transfers between devices with their start and end apart: 5, of which 4 were waited for; matrix products, arithmetic and copies ran while one was open for 4% of the time, Pallas kernels for 0%

profile of v1, /device:TPU:0, one launch (start us, length us, event | category | flops | bytes accessed | tf_op | source)
XLA Modules:
  0.0 541.2 jit_solution(17435254323299313925)
XLA Ops:
  6.5 0.0 all-gather.6.cloned.1.call-start
  6.5 0.7 all-gather.6.cloned.1.call-update
  7.3 0.0 all-gather.8.cloned.1.call-start
  7.3 5.5 %convert_reduce_fusion = f32[8192]{0:T(1024)S(1)} fusion(bf16[512,8192]{1,0:T(8,128)(2,1)} %param.3), kind=kLoop, calls=%fused_computation.1 | loop fusion | flops 8380416 | bytes 8421376 | tf_op jit(solution)/shard_map/reduce_sum | solution.py:198
  12.8 25.1 %all-gather = f32[131072]{0:T(1024)S(1)} all-gather(f32[8192]{0:T(1024)S(1)} %convert_reduce_fusion), channel_id=2, replica_groups=mesh['dp'=16,'feat'=8] {'dp'}, dimensions={0}, use_global_device_ids=true | all-gather | bytes 557056 | tf_op jit(solution)/shard_map/all_gather | solution.py:199
  37.8 0.1 reshape.132
  38.0 0.1 reduce_sum.135
  38.0 0.1 reduce-precision_convert_fusion.1
  38.1 26.1 %all-gather.6.cloned.1.call-done = bf16[8192,256]{1,0:T(8,128)(2,1)} async-done(((bf16[512,256]{1,0:T(8,128)(2,1)}), bf16[8192,256]{1,0:T(8,128)(2,1)}) %all-gather.6.cloned.1.call-update) | async-done | bytes 4194320 | tf_op jit(solution)/shard_map/all_gather | solution.py:197
  64.2 0.0 copy-start.3
  64.2 3.0 convolution_reduce_fusion
  67.3 0.4 copy-done.3
  67.7 6.4 %fusion.21 = bf16[512,256]{1,0:T(8,128)(2,1)} fusion(bf16[512,8192]{1,0:T(8,128)(2,1)} %param.3, bf16[8192,256]{1,0:T(8,128)(2,1)S(1)} %copy-done.3, f32[256]{0:T(256)S(1)} %broadcast_multiply_fusion), kind=kOutput, calls=%fused_computation.37 | convolution fusion | flops 2147745792 | bytes 12846080 | tf_op jit(solution)/shard_map/dot_general | solution.py:27
  74.1 0.0 all-gather.8.cloned.1.call-update
  74.1 0.0 all-gather.10.cloned.1.call-start
  74.2 27.3 %all-gather.8.cloned.1.call-done = bf16[512,2048]{1,0:T(8,128)(2,1)} async-done(((bf16[512,256]{1,0:T(8,128)(2,1)}), bf16[512,2048]{1,0:T(8,128)(2,1)}) %all-gather.8.cloned.1.call-update) | async-done | bytes 2097168 | tf_op jit(solution)/shard_map/all_gather | solution.py:202
  101.4 0.0 copy-start.1
  101.4 2.3 fusion.50
  103.7 0.0 copy-done.1
  103.7 0.0 copy-start.5
  103.7 0.5 fusion.52
  104.2 0.3 fusion.28
  104.5 24.9 %all_to_all.20 = f32[16,8,2176]{2,1,0:T(8,128)S(1)} all-to-all(f32[16,8,2176]{2,1,0:T(8,128)S(1)} %fusion.28), channel_id=1, replica_groups=mesh['dp'=16,'feat'=8] {'dp'}, dimensions={0} | all-to-all | bytes 2228224 | tf_op jit(solution)/shard_map/all_to_all | solution.py:168
  129.4 0.7 reduce_sum.138
  130.1 0.0 all-gather.10.cloned.1.call-update
  130.1 1.3 collective-permute-start
  131.4 0.0 copy-done.5
  131.4 2.0 convert_reduce_fusion.2
  133.3 60.9 %all-gather.1 = f32[32768]{0:T(1024)S(1)} all-gather(f32[2048]{0:T(1024)S(1)} %convert_reduce_fusion.2), channel_id=3, replica_groups=mesh['dp'=16,'feat'=8] {'dp'}, dimensions={0}, use_global_device_ids=true | all-gather | bytes 139264 | tf_op jit(solution)/shard_map/all_gather | solution.py:221
  194.4 0.0 collective-permute-done
  194.4 3.3 gather_fusion
  197.7 3.2 broadcast_select_fusion
  200.9 19.3 %all-gather.10.cloned.1.call-done = f32[1024,2176]{1,0:T(8,128)} async-done(((f32[8,2176]{1,0:T(8,128)}), f32[1024,2176]{1,0:T(8,128)}) %all-gather.10.cloned.1.call-update) | async-done | bytes 8912912 | tf_op jit(solution)/shard_map/all_gather | solution.py:215
  220.2 166.7 %shard_map.37 = bf16[2,2048,2048]{2,1,0:T(8,128)(2,1)} custom-call(f32[8,128,2176]{2,1,0:T(8,128)} %bitcast.53), custom_call_target="tpu_custom_call" | custom-call | tf_op jit(solution)/shard_map/pallas_call | solution.py:153
  386.8 0.0 copy-start
  386.8 0.0 copy-start.4
  386.8 7.7 %fusion.1 = f32[512,2048]{1,0:T(8,128)S(1)} fusion(bf16[512,2048]{1,0:T(8,128)(2,1)} %broadcast_select_fusion, bf16[2,2048,2048]{2,1,0:T(8,128)(2,1)} %shard_map.37), kind=kOutput, calls=%fused_computation.7 | convolution fusion | flops 4294967296 | bytes 14680064 | tf_op jit(solution)/shard_map/dot_general | solution.py:27
  394.5 1.1 copy-done
  395.7 0.6 copy-done.4
  396.3 0.0 copy-start.2
  396.3 6.2 %fusion.10 = f32[512,2048]{1,0:T(8,128)} fusion(f32[512,2048]{1,0:T(8,128)S(1)} %fusion.1, bf16[512,2048]{1,0:T(8,128)(2,1)S(1)} %copy-done.4, bf16[2,2048,2048]{2,1,0:T(8,128)(2,1)S(1)} %copy-done), kind=kOutput, calls=%fused_computation.21 | convolution fusion | flops 4296015872 | bytes 18874368 | tf_op jit(solution)/shard_map/dot_general | solution.py:27
  402.5 0.0 copy-done.2
  402.5 6.1 %fusion.2 = f32[512,2048]{1,0:T(8,128)} fusion(bf16[512,2048]{1,0:T(8,128)(2,1)S(1)} %copy-done.2, bf16[2,2048,2048]{2,1,0:T(8,128)(2,1)S(1)} %copy-done), kind=kOutput, calls=%fused_computation.8 | convolution fusion | flops 4294967296 | bytes 14680064 | tf_op jit(solution)/shard_map/dot_general | solution.py:27
  408.5 9.4 %fusion.7 = (f32[512]{0:T(512)S(1)}, f32[512]{0:T(512)S(1)}, f32[512]{0:T(512)S(1)}, f32[512,2048]{1,0:T(8,128)}) fusion(bf16[512,2048]{1,0:T(8,128)(2,1)} %broadcast_select_fusion, bf16[512,2048]{1,0:T(8,128)(2,1)S(1)} %copy-done.2, f32[512,2048]{1,0:T(8,128)} %fusion.10, f32[512,2048]{1,0:T(8,128)} %fusion.2, bf16[2,2048,2048]{2,1,0:T(8,128)(2,1)S(1)} %copy-done), kind=kOutput, calls=%fused_computation.17 | convolution fusion | flops 4304402944 | bytes 27269120 | tf_op jit(solution)/shard_map/dot_general | solution.py:27
  418.0 1.4 fusion.71
  419.4 0.8 fusion.11
  420.2 0.1 pad_maximum_fusion
  420.3 23.1 %all_to_all.21 = bf16[16,144,256]{2,1,0:T(8,128)(2,1)S(1)} all-to-all(bf16[16,144,256]{2,1,0:T(8,128)(2,1)S(1)} %pad_maximum_fusion), channel_id=1, replica_groups=mesh['dp'=16,'feat'=8] {'dp'}, dimensions={0} | all-to-all | bytes 2359296 | tf_op jit(solution)/shard_map/all_to_all | solution.py:168
  443.4 0.2 convert_reduce_fusion.3
  443.6 1.1 broadcast_in_dim.36
  444.7 3.9 all-to-all-start.2
  448.6 4.6 fusion
  453.2 4.6 fusion.25
  457.8 7.9 %all-to-all-done.2 = bf16[16,128,256]{2,1,0:T(8,128)(2,1)S(1)} async-done(((bf16[16,128,256]{2,1,0:T(8,128)(2,1)}), bf16[16,128,256]{2,1,0:T(8,128)(2,1)S(1)}, u32[]{:S(2)}, u32[]{:S(2)}) %all-to-all-start.2) | async-done | bytes 1048608 | tf_op jit(solution)/shard_map/all_to_all | solution.py:251
  465.7 0.3 multiply_reduce_fusion
  466.1 10.7 %convolution_convert_fusion = bf16[256,8192]{1,0:T(8,128)(2,1)} fusion(bf16[512,8192]{1,0:T(8,128)(2,1)} %param.3, f32[512,256]{1,0:T(8,128)S(1)} %get-tuple-element.15, bf16[2048,256]{1,0:T(8,128)(2,1)S(1)} %bitcast.52, f32[512,2048]{1,0:T(8,128)} %get-tuple-element.28, f32[256]{0:T(256)S(1)} %bitcast.59), kind=kOutput, calls=%fused_computation.2 | convolution fusion | flops 2687893504 | bytes 18351104 | tf_op jit(solution)/shard_map/dot_general | solution.py:27
  476.8 2.6 copy.13
  479.4 53.2 %all_to_all.22 = bf16[16,512,256]{1,2,0:T(8,128)(2,1)S(1)} all-to-all(bf16[16,512,256]{1,2,0:T(8,128)(2,1)S(1)} %bitcast.50), channel_id=1, replica_groups=mesh['dp'=16,'feat'=8] {'dp'}, dimensions={0} | all-to-all | bytes 8388608 | tf_op jit(solution)/shard_map/all_to_all | solution.py:168
  532.6 0.6 convert_reduce_fusion.1
  533.2 1.0 copy.9
  (14 shorter events, 0.2 us)
Async XLA Ops:
  6.5 57.7 %all-gather.6.cloned.1.call-start = ((), (), s32[]{:S(2)}) async-start(), calls=%async_computation.4 | async-start | bytes 4456448 | tf_op jit(solution)/shard_map/all_gather | solution.py:197
  7.3 94.2 %all-gather.8.cloned.1.call-start = ((), (), s32[]{:S(2)}) async-start(), calls=%async_computation.5 | async-start | bytes 2359296 | tf_op jit(solution)/shard_map/all_gather | solution.py:202
  64.2 3.4 copy-start.3
  74.1 146.1 %all-gather.10.cloned.1.call-start = ((), (), s32[]{:S(2)}) async-start(), calls=%async_computation.6 | async-start | bytes 8982528 | tf_op jit(solution)/shard_map/all_gather | solution.py:215
  101.4 2.3 copy-start.1
  103.7 27.6 %copy-start.5 = (s32[512]{0:T(512)S(1)}, s32[512]{0:T(512)}, u32[]{:S(2)}) copy-start(s32[512]{0:T(512)} %param.5) | copy-start | bytes 6148
  130.1 64.2 %collective-permute-start = (bf16[512,2048]{1,0:T(8,128)(2,1)}, bf16[512,2048]{1,0:T(8,128)(2,1)S(1)}, u32[]{:S(2)}, u32[]{:S(2)}) collective-permute-start(bf16[512,2048]{1,0:T(8,128)(2,1)} %all-gather.8.cloned.1.call-done), channel_id=1, source_target_pairs={{0,64},{8,72},{16,80},{24,88},{32,96},{40,104},{48,112},{56,120},{... | collective-permute-start | bytes 6291464 | tf_op jit(solution)/shard_map/ppermute | solution.py:18
  386.8 8.8 %copy-start = (bf16[2,2048,2048]{2,1,0:T(8,128)(2,1)S(1)}, bf16[2,2048,2048]{2,1,0:T(8,128)(2,1)}, u32[]{:S(2)}) copy-start(bf16[2,2048,2048]{2,1,0:T(8,128)(2,1)} %shard_map.37) | copy-start | bytes 50331652
  386.8 9.4 %copy-start.4 = (bf16[512,2048]{1,0:T(8,128)(2,1)S(1)}, bf16[512,2048]{1,0:T(8,128)(2,1)}, u32[]{:S(2)}) copy-start(bf16[512,2048]{1,0:T(8,128)(2,1)} %broadcast_select_fusion) | copy-start | bytes 6291460
  396.3 6.2 %copy-start.2 = (bf16[512,2048]{1,0:T(8,128)(2,1)S(1)}, bf16[512,2048]{1,0:T(8,128)(2,1)}, u32[]{:S(2)}) copy-start(bf16[512,2048]{1,0:T(8,128)(2,1)} %all-gather.8.cloned.1.call-done) | copy-start | bytes 6291460
  444.7 21.0 %all-to-all-start.2 = ((bf16[16,128,256]{2,1,0:T(8,128)(2,1)}), bf16[16,128,256]{2,1,0:T(8,128)(2,1)S(1)}, u32[]{:S(2)}, u32[]{:S(2)}) async-start(bf16[16,128,256]{2,1,0:T(8,128)(2,1)} %broadcast_in_dim.36), calls=%async_computation.2 | async-start | bytes 2097152 | tf_op jit(solution)/shard_map/all_to_all | solution.py:251
Sparse Core Ops, SparseCore 0:
  9.5 54.6 all-gather.5
  74.2 27.1 all-gather.7
  130.2 89.9 all-gather.9

commit v2 on v1

--- a/solution.py
+++ b/solution.py
@@ -31,7 +31,7 @@
     return jnp.dot(left, right, preferred_element_type=f32, precision=lax.Precision.HIGHEST)
 
 
-def invert_small(matrix):
+def invert_small(matrix, result):
     size = matrix.shape[0]
     groups = size // 8
     lane = lax.broadcasted_iota(jnp.int32, (8, size), 1)
@@ -64,24 +64,30 @@
                 )
             rows[i] = total
         rows[g] = panel
-    return jnp.concatenate(rows, axis=0)
-
-
-def invert_panel(block):
+        yield
+    result.append(jnp.concatenate(rows, axis=0))
+
+
+def invert_panel(block, result):
     half = block.shape[0] // 2
     b11, b12 = block[:half, :half], block[:half, half:]
     b21, b22 = block[half:, :half], block[half:, half:]
-    p1 = invert_small(b11)
+    found = []
+    yield from invert_small(b11, found)
+    p1 = found.pop()
     r1 = mat_high(p1, b12)
     low = mat_high(b21, p1)
-    p2 = invert_small(b22 - mat_high(b21, r1))
+    yield from invert_small(b22 - mat_high(b21, r1), found)
+    p2 = found.pop()
     q = mat_high(r1, p2)
     top = jnp.concatenate([p1 + mat_high(q, low), -q], axis=1)
     bottom = jnp.concatenate([-mat_high(p2, low), p2], axis=1)
-    return jnp.concatenate([top, bottom], axis=0)
-
-
-def inverse_kernel(batch_size, packed, out, work, left, right, fresh):
+    result.append(jnp.concatenate([top, bottom], axis=0))
+
+
+def inverse_kernel(
+    batch_size, which, packed, rows_in, rows_out, own_out, work, left, right, fresh, pivots
+):
     pairs, blk, _ = packed.shape
     blocks = 2 * pairs
     size = work.shape[0]
@@ -104,10 +110,14 @@
             work[a * blk : (a + 1) * blk, c * blk : (c + 1) * blk] = tile
             if c != a:
                 work[c * blk : (c + 1) * blk, a * blk : (a + 1) * blk] = tile.T
+    found = []
+    for _ in invert_panel(work[:wide, :wide], found):
+        pass
+    pivots[...] = found.pop()
 
     def step(k, carry):
         at_k = pl.ds(pl.multiple_of(k * wide, wide), wide)
-        pivot = invert_panel(work[at_k, at_k])
+        pivot = pivots[...]
         pivot_high, pivot_low = split_two(pivot)
         for i in range(steps):
             rows = slice(i * wide, (i + 1) * wide)
@@ -130,37 +140,63 @@
             right[2 * wide :, lanes] = low
         work[:, at_k] = jnp.zeros((size, wide), f32)
 
-        def update(j, inner):
-            lanes = pl.ds(pl.multiple_of(j * wide, wide), wide)
+        after = pl.ds(pl.multiple_of(jnp.minimum(k + 1, steps - 1) * wide, wide), wide)
+        coming = []
+        inversion = invert_panel(
+            work[after, after] - mat(left[after, :], right[:, after]), coming
+        )
+        for j in range(steps):
+            lanes = slice(j * wide, (j + 1) * wide)
             for part in range(2):
                 rows = slice(part * size // 2, (part + 1) * size // 2)
+                next(inversion, None)
+                next(inversion, None)
                 work[rows, lanes] = work[rows, lanes] - mat(left[rows, :], right[:, lanes])
-            return inner
-
-        lax.fori_loop(0, steps, update, 0)
+        for _ in inversion:
+            pass
+        pivots[...] = coming.pop()
         work[at_k, :] = fresh[...]
         return carry
 
     lax.fori_loop(0, steps, step, 0)
-    for i in range(steps):
-        rows = slice(i * wide, (i + 1) * wide)
-        high, low = split_two(work[rows, :])
-        out[0, rows, :] = high
-        out[1, rows, :] = low
-
-
-def inverse_parts(packed, size, batch_size, wide=256):
+
+    def apply(j, carry):
+        lanes = pl.ds(pl.multiple_of(j * wide, wide), wide)
+        high, low = split_two(work[:, lanes])
+        rows_out[:, lanes] = mat(rows_in[...], high) + mat(rows_in[...], low)
+        return carry
+
+    lax.fori_loop(0, steps, apply, 0)
+    own_cols = own_out.shape[2]
+    own_lanes = pl.ds(pl.multiple_of(which[0] * own_cols, own_cols), own_cols)
+    high, low = split_two(work[:, own_lanes])
+    own_out[0] = high
+    own_out[1] = low
+
+
+def apply_inverse(packed, rows, which, own_cols, batch_size, wide=256):
+    count, size = rows.shape
+    in_vmem = pl.BlockSpec(memory_space=pltpu.VMEM)
     return pl.pallas_call(
         lambda *refs: inverse_kernel(batch_size, *refs),
-        out_shape=jax.ShapeDtypeStruct((2, size, size), bf16),
+        out_shape=(
+            jax.ShapeDtypeStruct((count, size), f32),
+            jax.ShapeDtypeStruct((2, size, own_cols), bf16),
+        ),
+        in_specs=[pl.BlockSpec(memory_space=pltpu.SMEM), in_vmem, in_vmem],
+        out_specs=(in_vmem, in_vmem),
         scratch_shapes=[
             pltpu.VMEM((size, size), f32),
             pltpu.VMEM((size, 3 * wide), bf16),
             pltpu.VMEM((3 * wide, size), bf16),
             pltpu.VMEM((wide, size), f32),
+            pltpu.VMEM((wide, wide), f32),
         ],
         compiler_params=pltpu.CompilerParams(vmem_limit_bytes=60 * 2**20),
-    )(packed)
+        cost_estimate=pl.CostEstimate(
+            flops=150_000_000_000, bytes_accessed=20_000_000, transcendentals=0
+        ),
+    )(which, packed, rows)
 
 
 def sum_shares(array, axis):
@@ -201,7 +237,6 @@
     own_centered = (mat(features, weight) - col_mean).astype(bf16)
     centered = lax.all_gather(own_centered, "feat", axis=1, tiled=True)
 
-    received = from_behind(centered, "dp", dp_count // 2)
     first = mat(pick_cols(centered, feat_idx).T, centered)
     second = mat(pick_cols(centered, 2 * feat_count - 1 - feat_idx).T, centered)
     joined = jnp.concatenate([first, second], axis=1)
@@ -215,21 +250,26 @@
     packed = lax.all_gather(cov_share, ("feat", "dp"), axis=0, tiled=True)
     packed = packed.reshape(feat_count, blk_width, emb_width + blk_width)
 
-    local_pos = partner - (dp_idx + dp_count // 2) % dp_count * row_count
-    mates = jnp.take(received, local_pos, axis=0)
     center_sum = jnp.sum(centered.astype(f32), axis=0)
     center_sum = jnp.sum(lax.all_gather(center_sum, "dp"), axis=0)
-    sum_rows = three_parts(center_sum)
-    packed, mates, sum_rows = lax.optimization_barrier((packed, mates, sum_rows))
-
-    parts = inverse_parts(packed, emb_width, batch_size)
-    white_rows = mat(centered, parts[0]) + mat(centered, parts[1])
-    mate_white = mat(mates, parts[0]) + mat(mates, parts[1])
-    sum_white = jnp.sum(mat(sum_rows, parts[0]) + mat(sum_rows, parts[1]), axis=0)
-    mates_wide = mates.astype(f32)
+    all_rows = jnp.concatenate([centered, three_parts(center_sum)], axis=0)
+    packed, centered, all_rows = lax.optimization_barrier((packed, centered, all_rows))
+
+    received = from_behind(centered, "dp", dp_count // 2)
+    white_all, own_inverse = apply_inverse(
+        packed, all_rows, feat_idx.reshape(1), own_cols, batch_size
+    )
+    white_rows = white_all[:row_count]
+    sum_white = jnp.sum(white_all[row_count:], axis=0)
     norm_sq = jnp.sum(white_rows * centered.astype(f32), axis=1)
-    cross = jnp.sum(white_rows * mates_wide, axis=1)
-    mate_sq = jnp.sum(mate_white * mates_wide, axis=1)
+    local_pos = partner - (dp_idx + dp_count // 2) % dp_count * row_count
+    chosen = local_pos[:, None] == lax.broadcasted_iota(jnp.int32, (row_count, row_count), 1)
+    mates = mat(chosen.astype(bf16), received).astype(bf16)
+    mate_sq = jnp.sum(
+        jnp.where(chosen, from_behind(norm_sq, "dp", dp_count // 2)[None, :], 0.0), axis=1
+    )
+    mate_own = mat(mates, own_inverse[0]) + mat(mates, own_inverse[1])
+    cross = jnp.sum(white_rows * mates.astype(f32), axis=1)
     inv_norm = lax.rsqrt(norm_sq + norm_eps)
     mate_inv = lax.rsqrt(mate_sq + norm_eps)
     scale = 4.0 / math.sqrt(batch_size)
@@ -237,7 +277,7 @@
         cross * inv_norm * mate_inv + norm_eps * inv_norm * inv_norm
     )
     beta = -scale * inv_norm * mate_inv
-    own_back = alpha[:, None] * own(white_rows) + beta[:, None] * own(mate_white)
+    own_back = alpha[:, None] * own(white_rows) + beta[:, None] * mate_own
     own_sum = jnp.sum(own_back, axis=0)
 
     moment = mat(centered.T, own_back.astype(bf16)) / batch_size

time: 550 us -> 467 us (0.85)
  blocking collectives: 187 us -> 145 us
  Pallas kernels: 167 us -> 128 us
  matrix products: 62.2 us -> 31.3 us
  waiting for transfers between devices: 81.3 us -> 112 us
    all_gather x1, blocking collectives: 60.9 us -> 21.8 us  [body(): center_sum = jnp.sum(lax.all_gather(center_sum, 'dp'), axis=0)]
    pallas_call x1, Pallas kernels: 167 us -> 128 us  [apply_inverse(): pl.pallas_call(lambda *refs: inverse_kernel(batch_size, *refs), out_shape...]
    dot_general x12 -> x9, matrix products: 62.2 us -> 31.3 us  [mat(): return jnp.dot(left, right, preferred_element_type=f32)]
    all_gather x1, waiting for transfers between devices: 19.3 us -> 40.3 us  [body(): packed = lax.all_gather(cov_share, ('feat', 'dp'), axis=0, tiled=True)]
    all_to_all x1, waiting for transfers between devices: 7.92 us -> 14.7 us  [body(): lax.all_to_all(jnp.broadcast_to(moment_share, (dp_count,) + moment_share....]
  transfers between devices with their start and end apart: 5 -> 6, of which waited for: 4 -> 5; matrix products, arithmetic and copies ran while one was open for 4% -> 3% of each run, Pallas kernels for 0% -> 28%
where the time goes in v2:
time: 467 us; the launch traced here: 460 us
  blocking collectives  145 us (31%)
  Pallas kernels  128 us (27%)
  waiting for transfers between devices  112 us (24%)
  matrix products  31.3 us (7%)
  other arithmetic  17.6 us (4%)
  between operations  13.8 us (3%)
  starting transfers between devices  7.49 us (2%)
  local copies, waits for them, and re-layouts  5.28 us (1%)
    pallas_call x1, Pallas kernels, apply_inverse(): pl.pallas_call(lambda *refs: inverse_kernel(batch_size, *refs), out_shape...  128 us
    all_to_all x3, blocking collectives, sum_shares(): lax.all_to_all(array, axis, 0, 0, tiled=True).astype(f32)  98 us
    all_gather x1, waiting for transfers between devices, body(): packed = lax.all_gather(cov_share, ('feat', 'dp'), axis=0, tiled=True)  40.3 us
    dot_general x9, matrix products, mat(): return jnp.dot(left, right, preferred_element_type=f32)  31.3 us
    all_gather x1, waiting for transfers between devices, body(): centered = lax.all_gather(own_centered, 'feat', axis=1, tiled=True)  27.3 us
    all_gather x1, waiting for transfers between devices, body(): weight = lax.all_gather(proj_weight, 'dp', axis=0, tiled=True)  26.1 us
    all_gather x1, blocking collectives, body(): feature_sum = jnp.sum(lax.all_gather(feature_sum, 'dp'), axis=0)  25.1 us
    all_gather x1, blocking collectives, body(): center_sum = jnp.sum(lax.all_gather(center_sum, 'dp'), axis=0)  21.8 us
  transfers between devices with their start and end apart: 6, of which 5 were waited for; matrix products, arithmetic and copies ran while one was open for 3% of the time, Pallas kernels for 28%

profile of v2, /device:TPU:0, one launch (start us, length us, event | category | flops | bytes accessed | tf_op | source)
XLA Modules:
  0.0 460.1 jit_solution(8045919093580541031)
XLA Ops:
  6.5 0.0 all-gather.6.cloned.1.call-start
  6.5 0.7 all-gather.6.cloned.1.call-update
  7.3 0.0 all-gather.8.cloned.1.call-start
  7.3 5.5 %convert_reduce_fusion = f32[8192]{0:T(1024)S(1)} fusion(bf16[512,8192]{1,0:T(8,128)(2,1)} %param.3), kind=kLoop, calls=%fused_computation | loop fusion | flops 8380416 | bytes 8421376 | tf_op jit(solution)/shard_map/reduce_sum | solution.py:234
  12.8 25.1 %all-gather = f32[131072]{0:T(1024)S(1)} all-gather(f32[8192]{0:T(1024)S(1)} %convert_reduce_fusion), channel_id=2, replica_groups=mesh['dp'=16,'feat'=8] {'dp'}, dimensions={0}, use_global_device_ids=true | all-gather | bytes 557056 | tf_op jit(solution)/shard_map/all_gather | solution.py:235
  37.8 0.1 reshape.125
  38.0 0.1 reduce_sum.135
  38.0 0.1 reduce-precision_convert_fusion.1
  38.1 26.1 %all-gather.6.cloned.1.call-done = bf16[8192,256]{1,0:T(8,128)(2,1)} async-done(((bf16[512,256]{1,0:T(8,128)(2,1)}), bf16[8192,256]{1,0:T(8,128)(2,1)}) %all-gather.6.cloned.1.call-update) | async-done | bytes 4194320 | tf_op jit(solution)/shard_map/all_gather | solution.py:233
  64.2 0.0 copy-start.1
  64.2 3.0 convolution_reduce_fusion
  67.3 0.4 copy-done.1
  67.7 6.4 %fusion.11 = bf16[512,256]{1,0:T(8,128)(2,1)} fusion(bf16[512,8192]{1,0:T(8,128)(2,1)} %param.3, bf16[8192,256]{1,0:T(8,128)(2,1)S(1)} %copy-done.1, f32[256]{0:T(256)S(1)} %broadcast_multiply_fusion), kind=kOutput, calls=%fused_computation.25 | convolution fusion | flops 2147745792 | bytes 12846080 | tf_op jit(solution)/shard_map/dot_general | solution.py:27
  74.1 0.0 all-gather.8.cloned.1.call-update
  74.1 0.0 all-gather.10.cloned.1.call-start
  74.2 27.3 %all-gather.8.cloned.1.call-done = bf16[512,2048]{1,0:T(8,128)(2,1)} async-done(((bf16[512,256]{1,0:T(8,128)(2,1)}), bf16[512,2048]{1,0:T(8,128)(2,1)}) %all-gather.8.cloned.1.call-update) | async-done | bytes 2097168 | tf_op jit(solution)/shard_map/all_gather | solution.py:238
  101.4 2.2 fusion.45
  103.6 2.2 fusion.47
  105.7 0.3 fusion.17
  106.0 0.0 copy-start.3
  106.0 24.9 %all_to_all.20 = f32[16,8,2176]{2,1,0:T(8,128)S(1)} all-to-all(f32[16,8,2176]{2,1,0:T(8,128)S(1)} %fusion.17), channel_id=1, replica_groups=mesh['dp'=16,'feat'=8] {'dp'}, dimensions={0} | all-to-all | bytes 2228224 | tf_op jit(solution)/shard_map/all_to_all | solution.py:204
  130.9 0.7 reduce_sum.138
  131.6 0.0 all-gather.10.cloned.1.call-update
  131.6 0.0 copy-done.3
  131.7 0.6 broadcast_subtract_fusion
  132.3 2.0 convert_reduce_fusion.2
  134.2 21.8 %all-gather.1 = f32[32768]{0:T(1024)S(1)} all-gather(f32[2048]{0:T(1024)S(1)} %convert_reduce_fusion.2), channel_id=3, replica_groups=mesh['dp'=16,'feat'=8] {'dp'}, dimensions={0}, use_global_device_ids=true | all-gather | bytes 139264 | tf_op jit(solution)/shard_map/all_gather | solution.py:254
  156.1 3.2 pad_maximum_fusion.refs_2_
  159.3 40.3 %all-gather.10.cloned.1.call-done = f32[1024,2176]{1,0:T(8,128)} async-done(((f32[8,2176]{1,0:T(8,128)}), f32[1024,2176]{1,0:T(8,128)}) %all-gather.10.cloned.1.call-update) | async-done | bytes 8912912 | tf_op jit(solution)/shard_map/all_gather | solution.py:250
  199.6 1.8 collective-permute-start
  201.3 0.0 copy-start.2
  201.3 128.3 %shard_map.37 = (f32[528,2048]{1,0:T(8,128)}, bf16[2,2048,256]{2,1,0:T(8,128)(2,1)}) custom-call(s32[1]{0:T(128)} %bitcast.refs_0_, f32[8,128,2176]{2,1,0:T(8,128)} %bitcast.46, bf16[528,2048]{1,0:T(8,128)(2,1)} %pad_maximum_fusion.refs_2_), custom_call_target="tpu_custom_call" | custom-call | flops 149999992832 | bytes 20000000 | tf_op jit(solution)/shard_map/pallas_call | solution.py:180
  329.6 0.0 collective-permute-done
  329.6 0.0 copy-done.2
  329.7 0.0 copy-start
  329.7 3.0 convolution_convert_fusion.1
  332.7 0.0 copy-done
  332.7 0.0 copy-start.4
  332.7 2.8 multiply_reduce_fusion
  335.5 2.0 collective-permute-start.1
  337.5 0.0 copy-done.4
  337.5 0.7 fusion.20
  338.2 2.5 collective-permute-done.1
  340.7 0.2 select_reduce_fusion
  341.0 0.7 fusion.68
  341.7 2.4 fusion
  344.1 0.1 pad_maximum_fusion.1
  344.2 21.7 %all_to_all.21 = bf16[16,144,256]{2,1,0:T(8,128)(2,1)S(1)} all-to-all(bf16[16,144,256]{2,1,0:T(8,128)(2,1)S(1)} %pad_maximum_fusion.1), channel_id=1, replica_groups=mesh['dp'=16,'feat'=8] {'dp'}, dimensions={0} | all-to-all | bytes 2359296 | tf_op jit(solution)/shard_map/all_to_all | solution.py:204
  365.9 0.2 convert_reduce_fusion.3
  366.1 1.1 broadcast_in_dim.37
  367.2 3.7 all-to-all-start.2
  370.8 0.9 slice_reduce_fusion
  371.8 14.7 %all-to-all-done.2 = bf16[16,128,256]{2,1,0:T(8,128)(2,1)S(1)} async-done(((bf16[16,128,256]{2,1,0:T(8,128)(2,1)}), bf16[16,128,256]{2,1,0:T(8,128)(2,1)S(1)}, u32[]{:S(2)}, u32[]{:S(2)}) %all-to-all-start.2) | async-done | bytes 1048608 | tf_op jit(solution)/shard_map/all_to_all | solution.py:291
  386.5 0.3 multiply_reduce_fusion.2
  386.9 10.7 %convolution_convert_fusion = bf16[256,8192]{1,0:T(8,128)(2,1)} fusion(bf16[512,8192]{1,0:T(8,128)(2,1)} %param.3, f32[512,256]{1,0:T(8,128)S(1)} %get-tuple-element.29, bf16[2048,256]{1,0:T(8,128)(2,1)S(1)} %bitcast.38, f32[256]{0:T(256)S(1)} %bitcast.43, f32[528,2048]{1,0:T(8,128)} %get-tuple-element.12), kind=kOutput, calls=%fused_computation.1 | convolution fusion | flops 2686844928 | bytes 16253952 | tf_op jit(solution)/shard_map/dot_general | solution.py:27
  397.5 2.6 copy.13
  400.2 51.4 %all_to_all.22 = bf16[16,512,256]{1,2,0:T(8,128)(2,1)S(1)} all-to-all(bf16[16,512,256]{1,2,0:T(8,128)(2,1)S(1)} %bitcast.36), channel_id=1, replica_groups=mesh['dp'=16,'feat'=8] {'dp'}, dimensions={0} | all-to-all | bytes 8388608 | tf_op jit(solution)/shard_map/all_to_all | solution.py:204
  451.6 0.6 convert_reduce_fusion.1
  452.1 1.0 copy.9
  (12 shorter events, 0.2 us)
Async XLA Ops:
  6.5 57.7 %all-gather.6.cloned.1.call-start = ((), (), s32[]{:S(2)}) async-start(), calls=%async_computation.4 | async-start | bytes 4456448 | tf_op jit(solution)/shard_map/all_gather | solution.py:233
  7.3 94.2 %all-gather.8.cloned.1.call-start = ((), (), s32[]{:S(2)}) async-start(), calls=%async_computation.5 | async-start | bytes 2359296 | tf_op jit(solution)/shard_map/all_gather | solution.py:238
  64.2 3.4 copy-start.1
  74.1 125.5 %all-gather.10.cloned.1.call-start = ((), (), s32[]{:S(2)}) async-start(), calls=%async_computation.6 | async-start | bytes 8982528 | tf_op jit(solution)/shard_map/all_gather | solution.py:250
  106.0 25.6 %copy-start.3 = (s32[512]{0:T(512)S(1)}, s32[512]{0:T(512)}, u32[]{:S(2)}) copy-start(s32[512]{0:T(512)} %param.5) | copy-start | bytes 6148
  199.6 130.1 %collective-permute-start = (bf16[512,2048]{1,0:T(8,128)(2,1)}, bf16[512,2048]{1,0:T(8,128)(2,1)}, u32[]{:S(2)}, u32[]{:S(2)}) collective-permute-start(bf16[512,2048]{1,0:T(8,128)(2,1)} %all-gather.8.cloned.1.call-done), channel_id=1, source_target_pairs={{0,64},{8,72},{16,80},{24,88},{32,96},{40,104},{48,112},{56,120},{... | collective-permute-start | bytes 6291464 | tf_op jit(solution)/shard_map/ppermute | solution.py:18
  201.3 128.3 %copy-start.2 = (s32[512]{0:T(512)S(1)}, s32[512]{0:T(512)}, u32[]{:S(2)}) copy-start(s32[512]{0:T(512)} %broadcast_subtract_fusion) | copy-start | bytes 6148
  329.7 3.0 copy-start
  332.7 4.8 %copy-start.4 = (bf16[2,2048,256]{2,1,0:T(8,128)(2,1)S(1)}, bf16[2,2048,256]{2,1,0:T(8,128)(2,1)}, u32[]{:S(2)}) copy-start(bf16[2,2048,256]{2,1,0:T(8,128)(2,1)} %get-tuple-element.14) | copy-start | bytes 6291460
  335.5 5.2 %collective-permute-start.1 = (f32[512]{0:T(512)S(1)}, f32[512]{0:T(512)S(1)}, u32[]{:S(2)}, u32[]{:S(2)}) collective-permute-start(f32[512]{0:T(512)S(1)} %get-tuple-element.16), channel_id=1, source_target_pairs={{0,64},{8,72},{16,80},{24,88},{32,96},{40,104},{48,112},{56,120},{... | collective-permute-start | bytes 6152 | tf_op jit(solution)/shard_map/ppermute | solution.py:18
  367.2 19.3 %all-to-all-start.2 = ((bf16[16,128,256]{2,1,0:T(8,128)(2,1)}), bf16[16,128,256]{2,1,0:T(8,128)(2,1)S(1)}, u32[]{:S(2)}, u32[]{:S(2)}) async-start(bf16[16,128,256]{2,1,0:T(8,128)(2,1)} %broadcast_in_dim.37), calls=%async_computation.2 | async-start | bytes 2097152 | tf_op jit(solution)/shard_map/all_to_all | solution.py:291
Sparse Core Ops, SparseCore 0:
  9.5 54.6 all-gather.5
  74.2 27.1 all-gather.7
  131.8 67.7 all-gather.9

commit v3 on v2

--- a/solution.py
+++ b/solution.py
@@ -97,40 +97,64 @@
         jnp.int32, (blk, blk), 1
     )
     ridge_tile = jnp.where(diagonal, ridge, 0.0)
-    for a in range(blocks):
-        for c in range(a + 1):
-            if a < pairs:
-                tile = packed[a, :, c * blk : (c + 1) * blk]
-            else:
-                at = (blocks - a + c) * blk
-                tile = packed[blocks - 1 - a, :, at : at + blk]
-            tile = tile * (1.0 / batch_size)
-            if c == a:
-                tile = tile + ridge_tile
-            work[a * blk : (a + 1) * blk, c * blk : (c + 1) * blk] = tile
-            if c != a:
-                work[c * blk : (c + 1) * blk, a * blk : (a + 1) * blk] = tile.T
+
+    def unpack(a, c):
+        if a < pairs:
+            tile = packed[a, :, c * blk : (c + 1) * blk]
+        else:
+            at = (blocks - a + c) * blk
+            tile = packed[blocks - 1 - a, :, at : at + blk]
+        tile = tile * (1.0 / batch_size)
+        if c == a:
+            tile = tile + ridge_tile
+        work[a * blk : (a + 1) * blk, c * blk : (c + 1) * blk] = tile
+        if c != a:
+            work[c * blk : (c + 1) * blk, a * blk : (a + 1) * blk] = tile.T
+
+    tiles = [(a, c) for a in range(blocks) for c in range(a + 1)]
+    ahead = (wide // blk) * (wide // blk + 1) // 2
+    for a, c in tiles[:ahead]:
+        unpack(a, c)
     found = []
-    for _ in invert_panel(work[:wide, :wide], found):
+    inversion = invert_panel(work[:wide, :wide], found)
+    for at, (a, c) in enumerate(tiles[ahead:]):
+        if at % 4 == 0:
+            next(inversion, None)
+        unpack(a, c)
+    for _ in inversion:
         pass
     pivots[...] = found.pop()
 
-    def step(k, carry):
+    def sweep(k, look_ahead):
         at_k = pl.ds(pl.multiple_of(k * wide, wide), wide)
         pivot = pivots[...]
         pivot_high, pivot_low = split_two(pivot)
+
+        def scaled(lanes):
+            high, low = split_two(work[at_k, lanes])
+            return mat(pivot_high, high) + (mat(pivot_high, low) + mat(pivot_low, high))
+
+        coming = []
+        inversion = iter(())
+        if look_ahead:
+            after = pl.ds(pl.multiple_of((k + 1) * wide, wide), wide)
+            row_high, row_low = split_two(scaled(after))
+            col_high, col_low = split_two(work[after, at_k])
+            change = mat(col_high, row_high) + (mat(col_low, row_high) + mat(col_high, row_low))
+            inversion = invert_panel(work[after, after] - change, coming)
         for i in range(steps):
             rows = slice(i * wide, (i + 1) * wide)
             high, low = split_two(work[rows, at_k])
             left[rows, :wide] = high
             left[rows, wide : 2 * wide] = low
             left[rows, 2 * wide :] = high
+            if i % 2 == 0:
+                next(inversion, None)
         for j in range(steps):
             lanes = slice(j * wide, (j + 1) * wide)
-            high, low = split_two(work[at_k, lanes])
-            fresh[:, lanes] = mat(pivot_high, high) + (
-                mat(pivot_high, low) + mat(pivot_low, high)
-            )
+            fresh[:, lanes] = scaled(lanes)
+            if j % 2 == 0:
+                next(inversion, None)
         fresh[:, at_k] = pivot
         for j in range(steps):
             lanes = slice(j * wide, (j + 1) * wide)
@@ -138,27 +162,29 @@
             right[:wide, lanes] = high
             right[wide : 2 * wide, lanes] = high
             right[2 * wide :, lanes] = low
+            if j % 2 == 0:
+                next(inversion, None)
         work[:, at_k] = jnp.zeros((size, wide), f32)
-
-        after = pl.ds(pl.multiple_of(jnp.minimum(k + 1, steps - 1) * wide, wide), wide)
-        coming = []
-        inversion = invert_panel(
-            work[after, after] - mat(left[after, :], right[:, after]), coming
-        )
         for j in range(steps):
             lanes = slice(j * wide, (j + 1) * wide)
             for part in range(2):
                 rows = slice(part * size // 2, (part + 1) * size // 2)
                 next(inversion, None)
-                next(inversion, None)
+                if part:
+                    next(inversion, None)
                 work[rows, lanes] = work[rows, lanes] - mat(left[rows, :], right[:, lanes])
         for _ in inversion:
             pass
-        pivots[...] = coming.pop()
+        if look_ahead:
+            pivots[...] = coming.pop()
         work[at_k, :] = fresh[...]
+
+    def step(k, carry):
+        sweep(k, True)
         return carry
 
-    lax.fori_loop(0, steps, step, 0)
+    lax.fori_loop(0, steps - 1, step, 0)
+    sweep(steps - 1, False)
 
     def apply(j, carry):
         lanes = pl.ds(pl.multiple_of(j * wide, wide), wide)
@@ -233,6 +259,10 @@
     weight = lax.all_gather(proj_weight, "dp", axis=0, tiled=True)
     feature_sum = jnp.sum(features.astype(f32), axis=0)
     feature_sum = jnp.sum(lax.all_gather(feature_sum, "dp"), axis=0)
+    cuts = 2
+    by_owner = features.reshape(row_count, dp_count, cuts, -1)
+    turned = [by_owner[:, :, cut].reshape(row_count, -1).T for cut in range(cuts)]
+    feature_sum, *turned = lax.optimization_barrier((feature_sum, *turned))
     col_mean = jnp.sum(mat(three_parts(feature_sum), weight), axis=0) / batch_size
     own_centered = (mat(features, weight) - col_mean).astype(bf16)
     centered = lax.all_gather(own_centered, "feat", axis=1, tiled=True)
@@ -295,8 +325,11 @@
     sum_moment = jnp.sum(sum_white[:, None] * moment.astype(f32), axis=0)
     back_mean = (own_total - sum_moment) / batch_size
     back_proj = (back_center - back_mean).astype(bf16)
-    grad = mat(features.T, back_proj).astype(bf16)
-    return sum_shares(grad.reshape(dp_count, -1, own_cols), "dp")
+    grads = [
+        sum_shares(mat(part, back_proj).astype(bf16).reshape(dp_count, -1, own_cols), "dp")
+        for part in turned
+    ]
+    return jnp.concatenate(grads, axis=0)
 
 
 def solution(mesh):

time: 467 us -> 467 us (level)
  blocking collectives: 145 us -> 93.7 us
  waiting for transfers between devices: 112 us -> 142 us
  local copies, waits for them, and re-layouts: 5.28 us -> 20.1 us
  starting transfers between devices: 7.49 us -> 15.7 us
  Pallas kernels: 128 us -> 122 us
    all_to_all x3 -> x2, blocking collectives: 98 us -> 46.8 us  [sum_shares(): lax.all_to_all(array, axis, 0, 0, tiled=True).astype(f32)]
    all_to_all x0 -> x2, waiting for transfers between devices: none -> 49.4 us  [sum_shares(): lax.all_to_all(array, axis, 0, 0, tiled=True).astype(f32)]
    all_gather x1, waiting for transfers between devices: 26.1 us -> 7.75 us  [body(): weight = lax.all_gather(proj_weight, 'dp', axis=0, tiled=True)]
    unnamed x10 -> x13, local copies, waits for them, and re-layouts: 0.41 us -> 12.8 us
    all_to_all x0 -> x2, starting transfers between devices: none -> 8.16 us  [sum_shares(): lax.all_to_all(array, axis, 0, 0, tiled=True).astype(f32)]
    slice x0 -> x1, local copies, waits for them, and re-layouts: none -> 6.01 us  [body(): by_owner[:, :, cut].reshape(row_count, -1)]
    pallas_call x1, Pallas kernels: 128 us -> 122 us  [apply_inverse(): pl.pallas_call(lambda *refs: inverse_kernel(batch_size, *refs), out_shape...]
    dot_general x9 -> x11, matrix products: 31.3 us -> 31 us  [mat(): return jnp.dot(left, right, preferred_element_type=f32)]
  transfers between devices with their start and end apart: 6 -> 8, of which waited for: 5 -> 7; matrix products, arithmetic and copies ran while one was open for 3% -> 8% of each run, Pallas kernels for 28% -> 27%
where the time goes in v3:
time: 467 us; the launch traced here: 459 us
  waiting for transfers between devices  142 us (30%)
  Pallas kernels  122 us (26%)
  blocking collectives  93.7 us (20%)
  matrix products  31 us (7%)
  other arithmetic  20.2 us (4%)
  local copies, waits for them, and re-layouts  20.1 us (4%)
  starting transfers between devices  15.7 us (3%)
  between operations  13.6 us (3%)
    pallas_call x1, Pallas kernels, apply_inverse(): pl.pallas_call(lambda *refs: inverse_kernel(batch_size, *refs), out_shape...  122 us
    all_to_all x2, waiting for transfers between devices, sum_shares(): lax.all_to_all(array, axis, 0, 0, tiled=True).astype(f32)  49.4 us
    all_to_all x2, blocking collectives, sum_shares(): lax.all_to_all(array, axis, 0, 0, tiled=True).astype(f32)  46.8 us
    all_gather x1, waiting for transfers between devices, body(): packed = lax.all_gather(cov_share, ('feat', 'dp'), axis=0, tiled=True)  40.2 us
    dot_general x11, matrix products, mat(): return jnp.dot(left, right, preferred_element_type=f32)  31 us
    all_gather x1, waiting for transfers between devices, body(): centered = lax.all_gather(own_centered, 'feat', axis=1, tiled=True)  27.1 us
    all_gather x1, blocking collectives, body(): feature_sum = jnp.sum(lax.all_gather(feature_sum, 'dp'), axis=0)  25.2 us
    all_gather x1, blocking collectives, body(): center_sum = jnp.sum(lax.all_gather(center_sum, 'dp'), axis=0)  21.8 us
  transfers between devices with their start and end apart: 8, of which 7 were waited for; matrix products, arithmetic and copies ran while one was open for 8% of the time, Pallas kernels for 27%

profile of v3, /device:TPU:0, one launch (start us, length us, event | category | flops | bytes accessed | tf_op | source)
XLA Modules:
  0.0 458.9 jit_solution(11118595485970478587)
XLA Ops:
  6.5 0.0 all-gather.6.cloned.1.call-start
  6.5 0.7 all-gather.6.cloned.1.call-update
  7.3 0.0 all-gather.8.cloned.1.call-start
  7.3 12.0 %copy.6 = bf16[512,8192]{0,1:T(8,128)(2,1)} copy(bf16[512,8192]{1,0:T(8,128)(2,1)} %param.3) | data formatting | bytes 16777216 | tf_op args[0]
  19.3 5.7 %convert_reduce_fusion = f32[8192]{0:T(1024)S(1)} fusion(bf16[512,8192]{1,0:T(8,128)(2,1)} %param.3), kind=kLoop, calls=%fused_computation | loop fusion | flops 8380416 | bytes 8421376 | tf_op jit(solution)/shard_map/reduce_sum | solution.py:260
  24.9 25.2 %all-gather = f32[131072]{0:T(1024)S(1)} all-gather(f32[8192]{0:T(1024)S(1)} %convert_reduce_fusion), channel_id=2, replica_groups=mesh['dp'=16,'feat'=8] {'dp'}, dimensions={0}, use_global_device_ids=true | all-gather | bytes 557056 | tf_op jit(solution)/shard_map/all_gather | solution.py:261
  50.1 0.1 reshape.109
  50.2 0.1 reduce_sum.142
  50.3 6.0 %fusion.64 = (bf16[512,16,1,256]{0,3,2,1:T(8,128)(2,1)}, bf16[512,16,1,256]{0,3,2,1:T(8,128)(2,1)}) fusion(bf16[512,16,2,256]{0,3,2,1:T(8,128)(2,1)} %bitcast.42), kind=kLoop, calls=%fused_computation.103 | loop fusion | bytes 16777216 | tf_op jit(solution)/shard_map/slice | solution.py:264
  56.4 7.7 %all-gather.6.cloned.1.call-done = bf16[8192,256]{1,0:T(8,128)(2,1)} async-done(((bf16[512,256]{1,0:T(8,128)(2,1)}), bf16[8192,256]{1,0:T(8,128)(2,1)}) %all-gather.6.cloned.1.call-update) | async-done | bytes 4194320 | tf_op jit(solution)/shard_map/all_gather | solution.py:259
  64.2 3.0 convolution_reduce_fusion
  67.2 0.4 copy-done.1
  67.6 6.4 %fusion.11 = bf16[512,256]{1,0:T(8,128)(2,1)} fusion(bf16[512,8192]{1,0:T(8,128)(2,1)} %param.3, bf16[8192,256]{1,0:T(8,128)(2,1)S(1)} %copy-done.1, f32[256]{0:T(256)S(1)} %broadcast_multiply_fusion), kind=kOutput, calls=%fused_computation.26 | convolution fusion | flops 2147745792 | bytes 12846080 | tf_op jit(solution)/shard_map/dot_general | solution.py:27
  74.0 0.0 all-gather.8.cloned.1.call-update
  74.1 0.0 all-gather.10.cloned.1.call-start
  74.1 27.1 %all-gather.8.cloned.1.call-done = bf16[512,2048]{1,0:T(8,128)(2,1)} async-done(((bf16[512,256]{1,0:T(8,128)(2,1)}), bf16[512,2048]{1,0:T(8,128)(2,1)}) %all-gather.8.cloned.1.call-update) | async-done | bytes 2097168 | tf_op jit(solution)/shard_map/all_gather | solution.py:268
  101.2 2.2 fusion.42
  103.4 2.2 fusion.44
  105.5 0.3 fusion.17
  105.8 0.0 copy-start.4
  105.8 24.9 %all_to_all.25 = f32[16,8,2176]{2,1,0:T(8,128)S(1)} all-to-all(f32[16,8,2176]{2,1,0:T(8,128)S(1)} %fusion.17), channel_id=1, replica_groups=mesh['dp'=16,'feat'=8] {'dp'}, dimensions={0} | all-to-all | bytes 2228224 | tf_op jit(solution)/shard_map/all_to_all | solution.py:230
  130.7 0.7 reduce_sum.144
  131.4 0.0 all-gather.10.cloned.1.call-update
  131.4 0.0 copy-done.4
  131.4 0.6 broadcast_subtract_fusion
  132.0 2.0 convert_reduce_fusion.3
  134.0 21.8 %all-gather.1 = f32[32768]{0:T(1024)S(1)} all-gather(f32[2048]{0:T(1024)S(1)} %convert_reduce_fusion.3), channel_id=3, replica_groups=mesh['dp'=16,'feat'=8] {'dp'}, dimensions={0}, use_global_device_ids=true | all-gather | bytes 139264 | tf_op jit(solution)/shard_map/all_gather | solution.py:284
  155.9 3.3 pad_maximum_fusion.refs_2_
  159.1 40.2 %all-gather.10.cloned.1.call-done = f32[1024,2176]{1,0:T(8,128)} async-done(((f32[8,2176]{1,0:T(8,128)}), f32[1024,2176]{1,0:T(8,128)}) %all-gather.10.cloned.1.call-update) | async-done | bytes 8912912 | tf_op jit(solution)/shard_map/all_gather | solution.py:280
  199.3 1.8 collective-permute-start
  201.1 122.5 %shard_map.37 = (f32[528,2048]{1,0:T(8,128)}, bf16[2,2048,256]{2,1,0:T(8,128)(2,1)}) custom-call(s32[1]{0:T(128)} %bitcast.5.refs_0_, f32[8,128,2176]{2,1,0:T(8,128)} %bitcast.54, bf16[528,2048]{1,0:T(8,128)(2,1)} %pad_maximum_fusion.refs_2_), custom_call_target="tpu_custom_call" | custom-call | flops 149999992832 | bytes 20000000 | tf_op jit(solution)/shard_map/pallas_call | solution.py:206
  323.6 0.0 collective-permute-done
  323.6 0.0 copy-done.3
  323.6 3.0 convolution_convert_fusion.2
  326.7 0.0 copy-done
  326.7 0.0 copy-start.5
  326.7 2.8 multiply_reduce_fusion
  329.5 2.0 collective-permute-start.1
  331.5 0.0 copy-done.5
  331.5 0.7 fusion.20
  332.2 2.5 collective-permute-done.1
  334.7 0.2 select_reduce_fusion
  335.0 0.7 fusion.65
  335.7 2.4 fusion
  338.1 0.1 pad_maximum_fusion.1
  338.2 21.9 %all_to_all.26 = bf16[16,144,256]{2,1,0:T(8,128)(2,1)S(1)} all-to-all(bf16[16,144,256]{2,1,0:T(8,128)(2,1)S(1)} %pad_maximum_fusion.1), channel_id=1, replica_groups=mesh['dp'=16,'feat'=8] {'dp'}, dimensions={0} | all-to-all | bytes 2359296 | tf_op jit(solution)/shard_map/all_to_all | solution.py:230
  360.1 0.2 convert_reduce_fusion.4
  360.3 1.1 broadcast_in_dim.37
  361.3 3.7 all-to-all-start.2
  365.0 0.9 slice_reduce_fusion
  365.9 14.5 %all-to-all-done.2 = bf16[16,128,256]{2,1,0:T(8,128)(2,1)S(1)} async-done(((bf16[16,128,256]{2,1,0:T(8,128)(2,1)}), bf16[16,128,256]{2,1,0:T(8,128)(2,1)S(1)}, u32[]{:S(2)}, u32[]{:S(2)}) %all-to-all-start.2) | async-done | bytes 1048608 | tf_op jit(solution)/shard_map/all_to_all | solution.py:321
  380.4 0.3 multiply_reduce_fusion.2
  380.8 0.0 copy-start.2
  380.8 3.1 fusion.12
  383.8 0.4 copy-done.2
  384.2 2.5 convolution_convert_fusion.1
  386.8 3.7 all-to-all-start.3
  390.5 4.8 %convolution_convert_fusion = bf16[4096,256]{1,0:T(8,128)(2,1)} fusion(bf16[4096,512]{1,0:T(8,128)(2,1)} %bitcast.44, bf16[512,256]{1,0:T(8,128)(2,1)S(1)} %fusion.12), kind=kOutput, calls=%fused_computation.1 | convolution fusion | flops 1074790400 | bytes 6553600 | tf_op jit(solution)/shard_map/dot_general | solution.py:27
  395.3 22.6 %all-to-all-done.3 = bf16[16,256,256]{2,1,0:T(8,128)(2,1)S(1)} async-done(((bf16[16,256,256]{2,1,0:T(8,128)(2,1)}), bf16[16,256,256]{2,1,0:T(8,128)(2,1)S(1)}, u32[]{:S(2)}, u32[]{:S(2)}) %all-to-all-start.3) | async-done | bytes 2097184 | tf_op jit(solution)/shard_map/all_to_all | solution.py:230
  417.9 4.4 all-to-all-start.4
  422.3 0.3 convert_reduce_fusion.2
  422.6 26.8 %all-to-all-done.4 = bf16[16,256,256]{2,1,0:T(8,128)(2,1)} async-done(((bf16[16,256,256]{2,1,0:T(8,128)(2,1)}), bf16[16,256,256]{2,1,0:T(8,128)(2,1)}, u32[]{:S(2)}, u32[]{:S(2)}) %all-to-all-start.4) | async-done | bytes 2097184 | tf_op jit(solution)/shard_map/all_to_all | solution.py:230
  449.4 1.9 convert_reduce_fusion.1
  451.4 0.8 pad_maximum_fusion.2
  (19 shorter events, 0.3 us)
Async XLA Ops:
  6.5 57.6 %all-gather.6.cloned.1.call-start = ((), (), s32[]{:S(2)}) async-start(), calls=%async_computation.5 | async-start | bytes 4456448 | tf_op jit(solution)/shard_map/all_gather | solution.py:259
  7.3 93.9 %all-gather.8.cloned.1.call-start = ((), (), s32[]{:S(2)}) async-start(), calls=%async_computation.6 | async-start | bytes 2359296 | tf_op jit(solution)/shard_map/all_gather | solution.py:268
  64.2 3.4 copy-start.1
  74.1 125.3 %all-gather.10.cloned.1.call-start = ((), (), s32[]{:S(2)}) async-start(), calls=%async_computation.7 | async-start | bytes 8982528 | tf_op jit(solution)/shard_map/all_gather | solution.py:280
  105.8 25.6 %copy-start.4 = (s32[512]{0:T(512)S(1)}, s32[512]{0:T(512)}, u32[]{:S(2)}) copy-start(s32[512]{0:T(512)} %param.5) | copy-start | bytes 6148
  199.3 124.3 %collective-permute-start = (bf16[512,2048]{1,0:T(8,128)(2,1)}, bf16[512,2048]{1,0:T(8,128)(2,1)}, u32[]{:S(2)}, u32[]{:S(2)}) collective-permute-start(bf16[512,2048]{1,0:T(8,128)(2,1)} %all-gather.8.cloned.1.call-done), channel_id=1, source_target_pairs={{0,64},{8,72},{16,80},{24,88},{32,96},{40,104},{48,112},{56,120},{... | collective-permute-start | bytes 6291464 | tf_op jit(solution)/shard_map/ppermute | solution.py:18
  201.1 122.5 %copy-start.3 = (s32[512]{0:T(512)S(1)}, s32[512]{0:T(512)}, u32[]{:S(2)}) copy-start(s32[512]{0:T(512)} %broadcast_subtract_fusion) | copy-start | bytes 6148
  323.6 3.1 copy-start
  326.7 4.8 %copy-start.5 = (bf16[2,2048,256]{2,1,0:T(8,128)(2,1)S(1)}, bf16[2,2048,256]{2,1,0:T(8,128)(2,1)}, u32[]{:S(2)}) copy-start(bf16[2,2048,256]{2,1,0:T(8,128)(2,1)} %get-tuple-element.19) | copy-start | bytes 6291460
  329.5 5.2 %collective-permute-start.1 = (f32[512]{0:T(512)S(1)}, f32[512]{0:T(512)S(1)}, u32[]{:S(2)}, u32[]{:S(2)}) collective-permute-start(f32[512]{0:T(512)S(1)} %get-tuple-element.22), channel_id=1, source_target_pairs={{0,64},{8,72},{16,80},{24,88},{32,96},{40,104},{48,112},{56,120},{... | collective-permute-start | bytes 6152 | tf_op jit(solution)/shard_map/ppermute | solution.py:18
  361.3 19.1 %all-to-all-start.2 = ((bf16[16,128,256]{2,1,0:T(8,128)(2,1)}), bf16[16,128,256]{2,1,0:T(8,128)(2,1)S(1)}, u32[]{:S(2)}, u32[]{:S(2)}) async-start(bf16[16,128,256]{2,1,0:T(8,128)(2,1)} %broadcast_in_dim.37), calls=%async_computation.2 | async-start | bytes 2097152 | tf_op jit(solution)/shard_map/all_to_all | solution.py:321
  380.8 3.5 copy-start.2
  386.8 31.1 %all-to-all-start.3 = ((bf16[16,256,256]{2,1,0:T(8,128)(2,1)}), bf16[16,256,256]{2,1,0:T(8,128)(2,1)S(1)}, u32[]{:S(2)}, u32[]{:S(2)}) async-start(bf16[16,256,256]{2,1,0:T(8,128)(2,1)} %bitcast.47), calls=%async_computation.3 | async-start | bytes 4194304 | tf_op jit(solution)/shard_map/all_to_all | solution.py:230
  417.9 31.5 %all-to-all-start.4 = ((bf16[16,256,256]{2,1,0:T(8,128)(2,1)}), bf16[16,256,256]{2,1,0:T(8,128)(2,1)}, u32[]{:S(2)}, u32[]{:S(2)}) async-start(bf16[16,256,256]{2,1,0:T(8,128)(2,1)} %bitcast.46), calls=%async_computation.4 | async-start | bytes 4194304 | tf_op jit(solution)/shard_map/all_to_all | solution.py:230
Sparse Core Ops, SparseCore 0:
  9.5 54.6 all-gather.5
  74.2 26.9 all-gather.7
  131.5 67.7 all-gather.9

commit v4 on v3

--- a/solution.py
+++ b/solution.py
@@ -27,8 +27,10 @@
     return jnp.dot(left, right, preferred_element_type=f32)
 
 
-def mat_high(left, right):
-    return jnp.dot(left, right, preferred_element_type=f32, precision=lax.Precision.HIGHEST)
+def mat_fine(left, right):
+    left_high, left_low = split_two(left)
+    right_high, right_low = split_two(right)
+    return mat(left_high, right_high) + (mat(left_high, right_low) + mat(left_low, right_high))
 
 
 def invert_small(matrix, result):
@@ -75,13 +77,13 @@
     found = []
     yield from invert_small(b11, found)
     p1 = found.pop()
-    r1 = mat_high(p1, b12)
-    low = mat_high(b21, p1)
-    yield from invert_small(b22 - mat_high(b21, r1), found)
+    r1 = mat_fine(p1, b12)
+    low = mat_fine(b21, p1)
+    yield from invert_small(b22 - mat_fine(b21, r1), found)
     p2 = found.pop()
-    q = mat_high(r1, p2)
-    top = jnp.concatenate([p1 + mat_high(q, low), -q], axis=1)
-    bottom = jnp.concatenate([-mat_high(p2, low), p2], axis=1)
+    q = mat_fine(r1, p2)
+    top = jnp.concatenate([p1 + mat_fine(q, low), -q], axis=1)
+    bottom = jnp.concatenate([-mat_fine(p2, low), p2], axis=1)
     result.append(jnp.concatenate([top, bottom], axis=0))
 
 
@@ -259,10 +261,7 @@
     weight = lax.all_gather(proj_weight, "dp", axis=0, tiled=True)
     feature_sum = jnp.sum(features.astype(f32), axis=0)
     feature_sum = jnp.sum(lax.all_gather(feature_sum, "dp"), axis=0)
-    cuts = 2
-    by_owner = features.reshape(row_count, dp_count, cuts, -1)
-    turned = [by_owner[:, :, cut].reshape(row_count, -1).T for cut in range(cuts)]
-    feature_sum, *turned = lax.optimization_barrier((feature_sum, *turned))
+    feature_sum, turned = lax.optimization_barrier((feature_sum, features.T))
     col_mean = jnp.sum(mat(three_parts(feature_sum), weight), axis=0) / batch_size
     own_centered = (mat(features, weight) - col_mean).astype(bf16)
     centered = lax.all_gather(own_centered, "feat", axis=1, tiled=True)
@@ -325,11 +324,8 @@
     sum_moment = jnp.sum(sum_white[:, None] * moment.astype(f32), axis=0)
     back_mean = (own_total - sum_moment) / batch_size
     back_proj = (back_center - back_mean).astype(bf16)
-    grads = [
-        sum_shares(mat(part, back_proj).astype(bf16).reshape(dp_count, -1, own_cols), "dp")
-        for part in turned
-    ]
-    return jnp.concatenate(grads, axis=0)
+    grad = mat(turned, back_proj).astype(bf16)
+    return sum_shares(grad.reshape(dp_count, -1, own_cols), "dp")
 
 
 def solution(mesh):

time: 467 us -> 456 us (0.976)
  blocking collectives: 93.7 us -> 145 us
  waiting for transfers between devices: 142 us -> 111 us
  local copies, waits for them, and re-layouts: 20.1 us -> 1.71 us
  starting transfers between devices: 15.7 us -> 7.54 us
    all_to_all x2 -> x3, blocking collectives: 46.8 us -> 98.1 us  [sum_shares(): lax.all_to_all(array, axis, 0, 0, tiled=True).astype(f32)]
    all_to_all x2 -> x0, waiting for transfers between devices: 49.4 us -> none  [sum_shares(): lax.all_to_all(array, axis, 0, 0, tiled=True).astype(f32)]
    all_gather x1, waiting for transfers between devices: 7.75 us -> 26.1 us  [body(): weight = lax.all_gather(proj_weight, 'dp', axis=0, tiled=True)]
    unnamed x13 -> x10, local copies, waits for them, and re-layouts: 12.8 us -> 0.41 us
    all_to_all x2 -> x0, starting transfers between devices: 8.16 us -> none  [sum_shares(): lax.all_to_all(array, axis, 0, 0, tiled=True).astype(f32)]
    slice x1 -> x0, local copies, waits for them, and re-layouts: 6.01 us -> none  [body(): by_owner[:, :, cut].reshape(row_count, -1)]
    dot_general x11 -> x9, matrix products: 31 us -> 31.2 us  [mat(): return jnp.dot(left, right, preferred_element_type=f32)]
  transfers between devices with their start and end apart: 8 -> 6, of which waited for: 7 -> 5; matrix products, arithmetic and copies ran while one was open for 8% -> 3% of each run, Pallas kernels for 27% -> 27%
where the time goes in v4:
time: 456 us; the launch traced here: 449 us
  blocking collectives  145 us (32%)
  Pallas kernels  120 us (26%)
  waiting for transfers between devices  111 us (24%)
  matrix products  31.2 us (7%)
  other arithmetic  18.3 us (4%)
  between operations  13.6 us (3%)
  starting transfers between devices  7.54 us (2%)
    pallas_call x1, Pallas kernels, apply_inverse(): pl.pallas_call(lambda *refs: inverse_kernel(batch_size, *refs), out_shape...  120 us
    all_to_all x3, blocking collectives, sum_shares(): lax.all_to_all(array, axis, 0, 0, tiled=True).astype(f32)  98.1 us
    all_gather x1, waiting for transfers between devices, body(): packed = lax.all_gather(cov_share, ('feat', 'dp'), axis=0, tiled=True)  40.3 us
    dot_general x9, matrix products, mat(): return jnp.dot(left, right, preferred_element_type=f32)  31.2 us
    all_gather x1, waiting for transfers between devices, body(): centered = lax.all_gather(own_centered, 'feat', axis=1, tiled=True)  27.3 us
    all_gather x1, waiting for transfers between devices, body(): weight = lax.all_gather(proj_weight, 'dp', axis=0, tiled=True)  26.1 us
    all_gather x1, blocking collectives, body(): feature_sum = jnp.sum(lax.all_gather(feature_sum, 'dp'), axis=0)  25.1 us
    all_gather x1, blocking collectives, body(): center_sum = jnp.sum(lax.all_gather(center_sum, 'dp'), axis=0)  21.8 us
  transfers between devices with their start and end apart: 6, of which 5 were waited for; matrix products, arithmetic and copies ran while one was open for 3% of the time, Pallas kernels for 27%

profile of v4, /device:TPU:0, one launch (start us, length us, event | category | flops | bytes accessed | tf_op | source)
XLA Modules:
  0.0 449.0 jit_solution(16570629226033493093)
XLA Ops:
  6.5 0.0 all-gather.6.cloned.1.call-start
  6.5 0.7 all-gather.6.cloned.1.call-update
  7.3 0.0 all-gather.8.cloned.1.call-start
  7.3 5.5 %convert_reduce_fusion = f32[8192]{0:T(1024)S(1)} fusion(bf16[512,8192]{1,0:T(8,128)(2,1)} %param.3), kind=kLoop, calls=%fused_computation | loop fusion | flops 8380416 | bytes 8421376 | tf_op jit(solution)/shard_map/reduce_sum | solution.py:262
  12.8 25.1 %all-gather = f32[131072]{0:T(1024)S(1)} all-gather(f32[8192]{0:T(1024)S(1)} %convert_reduce_fusion), channel_id=2, replica_groups=mesh['dp'=16,'feat'=8] {'dp'}, dimensions={0}, use_global_device_ids=true | all-gather | bytes 557056 | tf_op jit(solution)/shard_map/all_gather | solution.py:263
  37.8 0.1 reshape.101
  38.0 0.1 reduce_sum.133
  38.1 26.1 %all-gather.6.cloned.1.call-done = bf16[8192,256]{1,0:T(8,128)(2,1)} async-done(((bf16[512,256]{1,0:T(8,128)(2,1)}), bf16[8192,256]{1,0:T(8,128)(2,1)}) %all-gather.6.cloned.1.call-update) | async-done | bytes 4194320 | tf_op jit(solution)/shard_map/all_gather | solution.py:261
  64.2 0.0 copy-start.1
  64.2 3.0 convolution_reduce_fusion
  67.3 0.4 copy-done.1
  67.7 6.4 %fusion.11 = bf16[512,256]{1,0:T(8,128)(2,1)} fusion(bf16[512,8192]{1,0:T(8,128)(2,1)} %param.3, bf16[8192,256]{1,0:T(8,128)(2,1)S(1)} %copy-done.1, f32[256]{0:T(256)S(1)} %broadcast_multiply_fusion), kind=kOutput, calls=%fused_computation.24 | convolution fusion | flops 2147745792 | bytes 12846080 | tf_op jit(solution)/shard_map/dot_general | solution.py:27
  74.1 0.0 all-gather.8.cloned.1.call-update
  74.1 0.0 all-gather.10.cloned.1.call-start
  74.2 27.3 %all-gather.8.cloned.1.call-done = bf16[512,2048]{1,0:T(8,128)(2,1)} async-done(((bf16[512,256]{1,0:T(8,128)(2,1)}), bf16[512,2048]{1,0:T(8,128)(2,1)}) %all-gather.8.cloned.1.call-update) | async-done | bytes 2097168 | tf_op jit(solution)/shard_map/all_gather | solution.py:267
  101.4 2.2 fusion.45
  103.6 2.2 fusion.47
  105.8 0.3 fusion.19
  106.0 0.0 copy-start.3
  106.0 24.9 %all_to_all.20 = f32[16,8,2176]{2,1,0:T(8,128)S(1)} all-to-all(f32[16,8,2176]{2,1,0:T(8,128)S(1)} %fusion.19), channel_id=1, replica_groups=mesh['dp'=16,'feat'=8] {'dp'}, dimensions={0} | all-to-all | bytes 2228224 | tf_op jit(solution)/shard_map/all_to_all | solution.py:232
  130.9 0.7 reduce_sum.135
  131.6 0.0 all-gather.10.cloned.1.call-update
  131.6 0.0 copy-done.3
  131.7 0.6 broadcast_subtract_fusion
  132.3 2.0 convert_reduce_fusion.2
  134.2 21.8 %all-gather.1 = f32[32768]{0:T(1024)S(1)} all-gather(f32[2048]{0:T(1024)S(1)} %convert_reduce_fusion.2), channel_id=3, replica_groups=mesh['dp'=16,'feat'=8] {'dp'}, dimensions={0}, use_global_device_ids=true | all-gather | bytes 139264 | tf_op jit(solution)/shard_map/all_gather | solution.py:283
  156.1 3.2 pad_maximum_fusion.refs_2_
  159.3 40.3 %all-gather.10.cloned.1.call-done = f32[1024,2176]{1,0:T(8,128)} async-done(((f32[8,2176]{1,0:T(8,128)}), f32[1024,2176]{1,0:T(8,128)}) %all-gather.10.cloned.1.call-update) | async-done | bytes 8912912 | tf_op jit(solution)/shard_map/all_gather | solution.py:279
  199.6 1.8 collective-permute-start
  201.4 0.0 copy-start.2
  201.4 120.5 %shard_map.37 = (f32[528,2048]{1,0:T(8,128)}, bf16[2,2048,256]{2,1,0:T(8,128)(2,1)}) custom-call(s32[1]{0:T(128)} %bitcast.1.refs_0_, f32[8,128,2176]{2,1,0:T(8,128)} %bitcast.41, bf16[528,2048]{1,0:T(8,128)(2,1)} %pad_maximum_fusion.refs_2_), custom_call_target="tpu_custom_call" | custom-call | flops 149999992832 | bytes 20000000 | tf_op jit(solution)/shard_map/pallas_call | solution.py:208
  321.8 0.0 collective-permute-done
  321.8 0.0 copy-done.2
  321.8 0.0 copy-start
  321.8 3.0 convolution_convert_fusion.1
  324.9 0.0 copy-done
  324.9 0.0 copy-start.4
  324.9 2.8 multiply_reduce_fusion
  327.7 2.0 collective-permute-start.1
  329.7 0.0 copy-done.4
  329.7 0.7 fusion.22
  330.4 2.4 collective-permute-done.1
  332.9 0.2 select_reduce_fusion
  333.1 0.8 fusion.68
  333.9 2.4 fusion
  336.3 0.1 pad_maximum_fusion.1
  336.4 21.9 %all_to_all.21 = bf16[16,144,256]{2,1,0:T(8,128)(2,1)S(1)} all-to-all(bf16[16,144,256]{2,1,0:T(8,128)(2,1)S(1)} %pad_maximum_fusion.1), channel_id=1, replica_groups=mesh['dp'=16,'feat'=8] {'dp'}, dimensions={0} | all-to-all | bytes 2359296 | tf_op jit(solution)/shard_map/all_to_all | solution.py:232
  358.3 0.2 convert_reduce_fusion.3
  358.5 1.1 broadcast_in_dim.37
  359.6 3.7 all-to-all-start.2
  363.2 0.9 slice_reduce_fusion
  364.2 14.5 %all-to-all-done.2 = bf16[16,128,256]{2,1,0:T(8,128)(2,1)S(1)} async-done(((bf16[16,128,256]{2,1,0:T(8,128)(2,1)}), bf16[16,128,256]{2,1,0:T(8,128)(2,1)S(1)}, u32[]{:S(2)}, u32[]{:S(2)}) %all-to-all-start.2) | async-done | bytes 1048608 | tf_op jit(solution)/shard_map/all_to_all | solution.py:320
  378.6 0.3 multiply_reduce_fusion.2
  379.0 10.6 %convolution_convert_fusion = bf16[8192,256]{1,0:T(8,128)(2,1)} fusion(bf16[8192,512]{0,1:T(8,128)(2,1)} %bitcast.32, f32[512,256]{1,0:T(8,128)S(1)} %get-tuple-element.33, bf16[2048,256]{1,0:T(8,128)(2,1)S(1)} %bitcast.34, f32[256]{0:T(256)S(1)} %bitcast.40, f32[528,2048]{1,0:T(8,128)} %get-tuple-element.16), kind=kOutput, calls=%fused_computation.1 | convolution fusion | flops 2686844928 | bytes 16253952 | tf_op jit(solution)/shard_map/dot_general | solution.py:27
  389.6 51.3 %all_to_all.22 = bf16[16,512,256]{2,1,0:T(8,128)(2,1)S(1)} all-to-all(bf16[16,512,256]{2,1,0:T(8,128)(2,1)} %bitcast.33), channel_id=1, replica_groups=mesh['dp'=16,'feat'=8] {'dp'}, dimensions={0} | all-to-all | bytes 8388608 | tf_op jit(solution)/shard_map/all_to_all | solution.py:232
  440.9 1.4 convert_reduce_fusion.1
  (16 shorter events, 0.3 us)
Async XLA Ops:
  6.5 57.7 %all-gather.6.cloned.1.call-start = ((), (), s32[]{:S(2)}) async-start(), calls=%async_computation.4 | async-start | bytes 4456448 | tf_op jit(solution)/shard_map/all_gather | solution.py:261
  7.3 94.2 %all-gather.8.cloned.1.call-start = ((), (), s32[]{:S(2)}) async-start(), calls=%async_computation.5 | async-start | bytes 2359296 | tf_op jit(solution)/shard_map/all_gather | solution.py:267
  64.2 3.4 copy-start.1
  74.1 125.5 %all-gather.10.cloned.1.call-start = ((), (), s32[]{:S(2)}) async-start(), calls=%async_computation.6 | async-start | bytes 8982528 | tf_op jit(solution)/shard_map/all_gather | solution.py:279
  106.0 25.6 %copy-start.3 = (s32[512]{0:T(512)S(1)}, s32[512]{0:T(512)}, u32[]{:S(2)}) copy-start(s32[512]{0:T(512)} %param.5) | copy-start | bytes 6148
  199.6 122.3 %collective-permute-start = (bf16[512,2048]{1,0:T(8,128)(2,1)}, bf16[512,2048]{1,0:T(8,128)(2,1)}, u32[]{:S(2)}, u32[]{:S(2)}) collective-permute-start(bf16[512,2048]{1,0:T(8,128)(2,1)} %all-gather.8.cloned.1.call-done), channel_id=1, source_target_pairs={{0,64},{8,72},{16,80},{24,88},{32,96},{40,104},{48,112},{56,120},{... | collective-permute-start | bytes 6291464 | tf_op jit(solution)/shard_map/ppermute | solution.py:18
  201.4 120.5 %copy-start.2 = (s32[512]{0:T(512)S(1)}, s32[512]{0:T(512)}, u32[]{:S(2)}) copy-start(s32[512]{0:T(512)} %broadcast_subtract_fusion) | copy-start | bytes 6148
  321.8 3.1 copy-start
  324.9 4.8 %copy-start.4 = (bf16[2,2048,256]{2,1,0:T(8,128)(2,1)S(1)}, bf16[2,2048,256]{2,1,0:T(8,128)(2,1)}, u32[]{:S(2)}) copy-start(bf16[2,2048,256]{2,1,0:T(8,128)(2,1)} %get-tuple-element.18) | copy-start | bytes 6291460
  327.7 5.2 %collective-permute-start.1 = (f32[512]{0:T(512)S(1)}, f32[512]{0:T(512)S(1)}, u32[]{:S(2)}, u32[]{:S(2)}) collective-permute-start(f32[512]{0:T(512)S(1)} %get-tuple-element.20), channel_id=1, source_target_pairs={{0,64},{8,72},{16,80},{24,88},{32,96},{40,104},{48,112},{56,120},{... | collective-permute-start | bytes 6152 | tf_op jit(solution)/shard_map/ppermute | solution.py:18
  359.6 19.1 %all-to-all-start.2 = ((bf16[16,128,256]{2,1,0:T(8,128)(2,1)}), bf16[16,128,256]{2,1,0:T(8,128)(2,1)S(1)}, u32[]{:S(2)}, u32[]{:S(2)}) async-start(bf16[16,128,256]{2,1,0:T(8,128)(2,1)} %broadcast_in_dim.37), calls=%async_computation.2 | async-start | bytes 2097152 | tf_op jit(solution)/shard_map/all_to_all | solution.py:320
Sparse Core Ops, SparseCore 0:
  9.5 54.6 all-gather.5
  74.2 27.1 all-gather.7
  131.8 67.7 all-gather.9

commit v5 on v4

--- a/solution.py
+++ b/solution.py
@@ -9,6 +9,7 @@
 
 ridge = 0.0001
 norm_eps = 1e-06
+pivot_width = 256
 f32 = jnp.float32
 bf16 = jnp.bfloat16
 
@@ -87,8 +88,27 @@
     result.append(jnp.concatenate([top, bottom], axis=0))
 
 
+def first_kernel(batch_size, total, out):
+    shape = total.shape
+    diagonal = lax.broadcasted_iota(jnp.int32, shape, 0) == lax.broadcasted_iota(
+        jnp.int32, shape, 1
+    )
+    found = []
+    for _ in invert_panel(total[...] * (1.0 / batch_size) + jnp.where(diagonal, ridge, 0.0), found):
+        pass
+    out[...] = found.pop()
+
+
+def first_pivot(total, batch_size):
+    return pl.pallas_call(
+        lambda *refs: first_kernel(batch_size, *refs),
+        out_shape=jax.ShapeDtypeStruct(total.shape, f32),
+        compiler_params=pltpu.CompilerParams(vmem_limit_bytes=16 * 2**20),
+    )(total)
+
+
 def inverse_kernel(
-    batch_size, which, packed, rows_in, rows_out, own_out, work, left, right, fresh, pivots
+    batch_size, which, packed, first, rows_in, rows_out, own_out, work, left, right, fresh, pivots
 ):
     pairs, blk, _ = packed.shape
     blocks = 2 * pairs
@@ -114,18 +134,9 @@
             work[c * blk : (c + 1) * blk, a * blk : (a + 1) * blk] = tile.T
 
     tiles = [(a, c) for a in range(blocks) for c in range(a + 1)]
-    ahead = (wide // blk) * (wide // blk + 1) // 2
-    for a, c in tiles[:ahead]:
+    for a, c in tiles:
         unpack(a, c)
-    found = []
-    inversion = invert_panel(work[:wide, :wide], found)
-    for at, (a, c) in enumerate(tiles[ahead:]):
-        if at % 4 == 0:
-            next(inversion, None)
-        unpack(a, c)
-    for _ in inversion:
-        pass
-    pivots[...] = found.pop()
+    pivots[...] = first[...]
 
     def sweep(k, look_ahead):
         at_k = pl.ds(pl.multiple_of(k * wide, wide), wide)
@@ -202,7 +213,7 @@
     own_out[1] = low
 
 
-def apply_inverse(packed, rows, which, own_cols, batch_size, wide=256):
+def apply_inverse(packed, first, rows, which, own_cols, batch_size, wide=pivot_width):
     count, size = rows.shape
     in_vmem = pl.BlockSpec(memory_space=pltpu.VMEM)
     return pl.pallas_call(
@@ -211,7 +222,7 @@
             jax.ShapeDtypeStruct((count, size), f32),
             jax.ShapeDtypeStruct((2, size, own_cols), bf16),
         ),
-        in_specs=[pl.BlockSpec(memory_space=pltpu.SMEM), in_vmem, in_vmem],
+        in_specs=[pl.BlockSpec(memory_space=pltpu.SMEM), in_vmem, in_vmem, in_vmem],
         out_specs=(in_vmem, in_vmem),
         scratch_shapes=[
             pltpu.VMEM((size, size), f32),
@@ -224,7 +235,7 @@
         cost_estimate=pl.CostEstimate(
             flops=150_000_000_000, bytes_accessed=20_000_000, transcendentals=0
         ),
-    )(which, packed, rows)
+    )(which, packed, first, rows)
 
 
 def sum_shares(array, axis):
@@ -261,7 +272,6 @@
     weight = lax.all_gather(proj_weight, "dp", axis=0, tiled=True)
     feature_sum = jnp.sum(features.astype(f32), axis=0)
     feature_sum = jnp.sum(lax.all_gather(feature_sum, "dp"), axis=0)
-    feature_sum, turned = lax.optimization_barrier((feature_sum, features.T))
     col_mean = jnp.sum(mat(three_parts(feature_sum), weight), axis=0) / batch_size
     own_centered = (mat(features, weight) - col_mean).astype(bf16)
     centered = lax.all_gather(own_centered, "feat", axis=1, tiled=True)
@@ -276,17 +286,26 @@
     cov_share = sum_shares(
         cov_pack.reshape(dp_count, blk_width // dp_count, emb_width + blk_width), "dp"
     )
+    lead = centered[:, :pivot_width]
+    cov_share, lead_part = lax.optimization_barrier((cov_share, mat(lead.T, lead)))
+    lead_share = sum_shares(lead_part.reshape(dp_count, -1, pivot_width), "dp")
+    lead_total = lax.all_to_all(
+        jnp.broadcast_to(lead_share, (dp_count,) + lead_share.shape), "dp", 0, 0, tiled=True
+    ).reshape(pivot_width, pivot_width)
+    first = first_pivot(lead_total, batch_size)
     packed = lax.all_gather(cov_share, ("feat", "dp"), axis=0, tiled=True)
     packed = packed.reshape(feat_count, blk_width, emb_width + blk_width)
 
     center_sum = jnp.sum(centered.astype(f32), axis=0)
     center_sum = jnp.sum(lax.all_gather(center_sum, "dp"), axis=0)
     all_rows = jnp.concatenate([centered, three_parts(center_sum)], axis=0)
-    packed, centered, all_rows = lax.optimization_barrier((packed, centered, all_rows))
+    packed, first, centered, all_rows = lax.optimization_barrier(
+        (packed, first, centered, all_rows)
+    )
 
     received = from_behind(centered, "dp", dp_count // 2)
     white_all, own_inverse = apply_inverse(
-        packed, all_rows, feat_idx.reshape(1), own_cols, batch_size
+        packed, first, all_rows, feat_idx.reshape(1), own_cols, batch_size
     )
     white_rows = white_all[:row_count]
     sum_white = jnp.sum(white_all[row_count:], axis=0)
@@ -324,7 +343,7 @@
     sum_moment = jnp.sum(sum_white[:, None] * moment.astype(f32), axis=0)
     back_mean = (own_total - sum_moment) / batch_size
     back_proj = (back_center - back_mean).astype(bf16)
-    grad = mat(turned, back_proj).astype(bf16)
+    grad = mat(features.T, back_proj).astype(bf16)
     return sum_shares(grad.reshape(dp_count, -1, own_cols), "dp")
 
 

time: 456 us -> 453 us (level)
  blocking collectives: 145 us -> 119 us
  starting transfers between devices: 7.54 us -> 23.2 us
  local copies, waits for them, and re-layouts: 1.71 us -> 6.7 us
    all_gather x1, waiting for transfers between devices: 40.3 us -> 8.39 us  [body(): packed = lax.all_gather(cov_share, ('feat', 'dp'), axis=0, tiled=True)]
    all_to_all x0 -> x3, waiting for transfers between devices: none -> 30.8 us  [the longest x2 25.4 us: sum_shares(): lax.all_to_all(array, axis, 0, 0, tiled=True).astype(f32)]
    all_to_all x3 -> x2, blocking collectives: 98.1 us -> 73.1 us  [sum_shares(): lax.all_to_all(array, axis, 0, 0, tiled=True).astype(f32)]
    all_to_all x0 -> x3, starting transfers between devices: none -> 15.8 us  [the longest x2 12 us: sum_shares(): lax.all_to_all(array, axis, 0, 0, tiled=True).astype(f32)]
    pallas_call x0 -> x1, Pallas kernels: none -> 8.6 us  [first_pivot(): pl.pallas_call(lambda *refs: first_kernel(batch_size, *refs), out_shape=j...]
    pallas_call x1, Pallas kernels: 120 us -> 112 us  [apply_inverse(): pl.pallas_call(lambda *refs: inverse_kernel(batch_size, *refs), out_shape...]
    dot_general x9 -> x10, matrix products: 31.2 us -> 33.3 us  [mat(): return jnp.dot(left, right, preferred_element_type=f32)]
  transfers between devices with their start and end apart: 6 -> 9, of which waited for: 5 -> 8; matrix products, arithmetic and copies ran while one was open for 3% -> 4% of each run, Pallas kernels for 27% -> 27%
where the time goes in v5:
time: 453 us; the launch traced here: 446 us
  Pallas kernels  121 us (27%)
  blocking collectives  119 us (26%)
  waiting for transfers between devices  110 us (24%)
  matrix products  33.3 us (7%)
  starting transfers between devices  23.2 us (5%)
  other arithmetic  18.6 us (4%)
  between operations  13.6 us (3%)
  local copies, waits for them, and re-layouts  6.7 us (1%)
    pallas_call x1, Pallas kernels, apply_inverse(): pl.pallas_call(lambda *refs: inverse_kernel(batch_size, *refs), out_shape...  112 us
    all_to_all x2, blocking collectives, sum_shares(): lax.all_to_all(array, axis, 0, 0, tiled=True).astype(f32)  73.1 us
    dot_general x10, matrix products, mat(): return jnp.dot(left, right, preferred_element_type=f32)  33.3 us
    all_gather x1, waiting for transfers between devices, body(): centered = lax.all_gather(own_centered, 'feat', axis=1, tiled=True)  27.3 us
    all_gather x1, waiting for transfers between devices, body(): weight = lax.all_gather(proj_weight, 'dp', axis=0, tiled=True)  26.1 us
    all_to_all x2, waiting for transfers between devices, sum_shares(): lax.all_to_all(array, axis, 0, 0, tiled=True).astype(f32)  25.4 us
    all_gather x1, blocking collectives, body(): feature_sum = jnp.sum(lax.all_gather(feature_sum, 'dp'), axis=0)  25.1 us
    all_gather x1, blocking collectives, body(): center_sum = jnp.sum(lax.all_gather(center_sum, 'dp'), axis=0)  21.1 us
  transfers between devices with their start and end apart: 9, of which 8 were waited for; matrix products, arithmetic and copies ran while one was open for 4% of the time, Pallas kernels for 27%

profile of v5, /device:TPU:0, one launch (start us, length us, event | category | flops | bytes accessed | tf_op | source)
XLA Modules:
  0.0 445.6 jit_solution(11098570612362376577)
XLA Ops:
  6.5 0.0 all-gather.6.cloned.1.call-start
  6.5 0.7 all-gather.6.cloned.1.call-update
  7.3 0.0 all-gather.8.cloned.1.call-start
  7.3 5.5 %convert_reduce_fusion = f32[8192]{0:T(1024)S(1)} fusion(bf16[512,8192]{1,0:T(8,128)(2,1)} %param.3), kind=kLoop, calls=%fused_computation | loop fusion | flops 8380416 | bytes 8421376 | tf_op jit(solution)/shard_map/reduce_sum | solution.py:273
  12.8 25.1 %all-gather = f32[131072]{0:T(1024)S(1)} all-gather(f32[8192]{0:T(1024)S(1)} %convert_reduce_fusion), channel_id=2, replica_groups=mesh['dp'=16,'feat'=8] {'dp'}, dimensions={0}, use_global_device_ids=true | all-gather | bytes 557056 | tf_op jit(solution)/shard_map/all_gather | solution.py:274
  37.8 0.1 reshape.133
  38.0 0.1 reduce_sum.144
  38.0 0.1 reduce-precision_convert_fusion.1
  38.1 26.1 %all-gather.6.cloned.1.call-done = bf16[8192,256]{1,0:T(8,128)(2,1)} async-done(((bf16[512,256]{1,0:T(8,128)(2,1)}), bf16[8192,256]{1,0:T(8,128)(2,1)}) %all-gather.6.cloned.1.call-update) | async-done | bytes 4194320 | tf_op jit(solution)/shard_map/all_gather | solution.py:272
  64.2 3.0 convolution_reduce_fusion
  67.3 0.4 copy-done.2
  67.7 6.4 %fusion.11 = bf16[512,256]{1,0:T(8,128)(2,1)} fusion(bf16[512,8192]{1,0:T(8,128)(2,1)} %param.3, bf16[8192,256]{1,0:T(8,128)(2,1)S(1)} %copy-done.2, f32[256]{0:T(256)S(1)} %broadcast_multiply_fusion), kind=kOutput, calls=%fused_computation.25 | convolution fusion | flops 2147745792 | bytes 12846080 | tf_op jit(solution)/shard_map/dot_general | solution.py:28
  74.1 0.0 all-gather.8.cloned.1.call-update
  74.1 27.3 %all-gather.8.cloned.1.call-done = bf16[512,2048]{1,0:T(8,128)(2,1)} async-done(((bf16[512,256]{1,0:T(8,128)(2,1)}), bf16[512,2048]{1,0:T(8,128)(2,1)}) %all-gather.8.cloned.1.call-update) | async-done | bytes 2097168 | tf_op jit(solution)/shard_map/all_gather | solution.py:277
  101.4 2.1 fusion.47
  103.6 2.2 fusion.49
  105.7 1.2 fusion.17
  107.0 6.9 %all-to-all-start = ((f32[16,8,2176]{2,1,0:T(8,128)}), f32[16,8,2176]{2,1,0:T(8,128)S(1)}, u32[]{:S(2)}, u32[]{:S(2)}) async-start(f32[16,8,2176]{2,1,0:T(8,128)} %fusion.17), calls=%async_computation | async-start | bytes 2228224 | tf_op jit(solution)/shard_map/all_to_all | solution.py:243
  113.9 0.0 all-gather.10.cloned.1.call-start
  114.0 2.1 fusion.35
  116.1 16.7 %all-to-all-done = f32[16,8,2176]{2,1,0:T(8,128)S(1)} async-done(((f32[16,8,2176]{2,1,0:T(8,128)}), f32[16,8,2176]{2,1,0:T(8,128)S(1)}, u32[]{:S(2)}, u32[]{:S(2)}) %all-to-all-start) | async-done | bytes 1114144 | tf_op jit(solution)/shard_map/all_to_all | solution.py:243
  132.8 0.7 reduce_sum.147
  133.5 0.0 all-gather.10.cloned.1.call-update
  133.5 0.0 copy-done.4
  133.5 0.6 broadcast_subtract_fusion
  134.1 2.0 convert_reduce_fusion.2
  136.1 21.1 %all-gather.1 = f32[32768]{0:T(1024)S(1)} all-gather(f32[2048]{0:T(1024)S(1)} %convert_reduce_fusion.2), channel_id=3, replica_groups=mesh['dp'=16,'feat'=8] {'dp'}, dimensions={0}, use_global_device_ids=true | all-gather | bytes 139264 | tf_op jit(solution)/shard_map/all_gather | solution.py:300
  157.2 5.1 %all-to-all-start.1 = ((f32[16,16,256]{2,1,0:T(8,128)}), f32[16,16,256]{2,1,0:T(8,128)S(1)}, u32[]{:S(2)}, u32[]{:S(2)}) async-start(f32[16,16,256]{2,1,0:T(8,128)} %bitcast.4), calls=%async_computation.1 | async-start | bytes 524288 | tf_op jit(solution)/shard_map/all_to_all | solution.py:243
  162.4 8.6 %all-to-all-done.1 = f32[16,16,256]{2,1,0:T(8,128)S(1)} async-done(((f32[16,16,256]{2,1,0:T(8,128)}), f32[16,16,256]{2,1,0:T(8,128)S(1)}, u32[]{:S(2)}, u32[]{:S(2)}) %all-to-all-start.1) | async-done | bytes 262176 | tf_op jit(solution)/shard_map/all_to_all | solution.py:243
  171.0 0.7 broadcast_in_dim.37
  171.7 3.8 all-to-all-start.2
  175.6 3.2 pad_maximum_fusion.refs_3_
  178.7 5.5 %all-to-all-done.2 = f32[16,16,256]{2,1,0:T(8,128)S(1)} async-done(((f32[16,16,256]{2,1,0:T(8,128)}), f32[16,16,256]{2,1,0:T(8,128)S(1)}, u32[]{:S(2)}, u32[]{:S(2)}) %all-to-all-start.2) | async-done | bytes 262176 | tf_op jit(solution)/shard_map/all_to_all | solution.py:292
  184.2 8.6 %shard_map.37.refs_2_ = f32[256,256]{1,0:T(8,128)S(1)} custom-call(f32[256,256]{1,0:T(8,128)S(1)} %bitcast.38), custom_call_target="tpu_custom_call" | custom-call | tf_op jit(solution)/shard_map/pallas_call | solution.py:103
  192.8 0.0 copy-start
  192.8 0.7 copy-done
  193.5 8.4 %all-gather.10.cloned.1.call-done = f32[1024,2176]{1,0:T(8,128)} async-done(((f32[8,2176]{1,0:T(8,128)}), f32[1024,2176]{1,0:T(8,128)}) %all-gather.10.cloned.1.call-update) | async-done | bytes 8912912 | tf_op jit(solution)/shard_map/all_gather | solution.py:296
  201.9 1.5 collective-permute-start
  203.4 112.2 %shard_map.38 = (f32[528,2048]{1,0:T(8,128)}, bf16[2,2048,256]{2,1,0:T(8,128)(2,1)}) custom-call(s32[1]{0:T(128)} %bitcast.refs_0_, f32[8,128,2176]{2,1,0:T(8,128)} %bitcast.49, f32[256,256]{1,0:T(8,128)} %copy-done, bf16[528,2048]{1,0:T(8,128)(2,1)} %pad_maximum_fusion.refs_3_), custom_call_target="tpu_custom_call" | custom-call | flops 149999992832 | bytes 20000000 | tf_op jit(solution)/shard_map/pallas_call | solution.py:219
  315.7 0.0 collective-permute-done
  315.7 0.0 copy-done.3
  315.7 3.0 convolution_convert_fusion.1
  318.7 0.0 copy-done.1
  318.7 0.0 copy-start.5
  318.7 2.8 multiply_reduce_fusion
  321.6 2.1 collective-permute-start.1
  323.7 0.7 fusion.20
  324.4 2.4 collective-permute-done.1
  326.7 0.2 select_reduce_fusion
  327.0 0.7 fusion.70
  327.7 2.4 fusion
  330.1 0.1 pad_maximum_fusion.1
  330.2 21.9 %all_to_all.30 = bf16[16,144,256]{2,1,0:T(8,128)(2,1)S(1)} all-to-all(bf16[16,144,256]{2,1,0:T(8,128)(2,1)S(1)} %pad_maximum_fusion.1), channel_id=1, replica_groups=mesh['dp'=16,'feat'=8] {'dp'}, dimensions={0} | all-to-all | bytes 2359296 | tf_op jit(solution)/shard_map/all_to_all | solution.py:243
  352.2 0.2 convert_reduce_fusion.3
  352.3 1.1 broadcast_in_dim.41
  353.4 3.7 all-to-all-start.4
  357.1 0.9 slice_reduce_fusion
  358.0 14.5 %all-to-all-done.4 = bf16[16,128,256]{2,1,0:T(8,128)(2,1)S(1)} async-done(((bf16[16,128,256]{2,1,0:T(8,128)(2,1)}), bf16[16,128,256]{2,1,0:T(8,128)(2,1)S(1)}, u32[]{:S(2)}, u32[]{:S(2)}) %all-to-all-start.4) | async-done | bytes 1048608 | tf_op jit(solution)/shard_map/all_to_all | solution.py:339
  372.5 0.3 multiply_reduce_fusion.2
  372.8 10.7 %convolution_convert_fusion = bf16[256,8192]{1,0:T(8,128)(2,1)} fusion(bf16[512,8192]{1,0:T(8,128)(2,1)} %param.3, f32[512,256]{1,0:T(8,128)S(1)} %get-tuple-element.35, bf16[2048,256]{1,0:T(8,128)(2,1)S(1)} %bitcast.41, f32[256]{0:T(256)S(1)} %bitcast.46, f32[528,2048]{1,0:T(8,128)} %get-tuple-element.18), kind=kOutput, calls=%fused_computation.1 | convolution fusion | flops 2686844928 | bytes 16253952 | tf_op jit(solution)/shard_map/dot_general | solution.py:28
  383.5 2.6 copy.13
  386.1 51.1 %all_to_all.31 = bf16[16,512,256]{1,2,0:T(8,128)(2,1)S(1)} all-to-all(bf16[16,512,256]{1,2,0:T(8,128)(2,1)S(1)} %bitcast.39), channel_id=1, replica_groups=mesh['dp'=16,'feat'=8] {'dp'}, dimensions={0} | all-to-all | bytes 8388608 | tf_op jit(solution)/shard_map/all_to_all | solution.py:243
  437.3 0.6 convert_reduce_fusion.1
  437.9 1.0 copy.9
  (18 shorter events, 0.2 us)
Async XLA Ops:
  6.5 57.7 %all-gather.6.cloned.1.call-start = ((), (), s32[]{:S(2)}) async-start(), calls=%async_computation.6 | async-start | bytes 4456448 | tf_op jit(solution)/shard_map/all_gather | solution.py:272
  7.3 94.2 %all-gather.8.cloned.1.call-start = ((), (), s32[]{:S(2)}) async-start(), calls=%async_computation.7 | async-start | bytes 2359296 | tf_op jit(solution)/shard_map/all_gather | solution.py:277
  64.2 3.4 copy-start.2
  107.0 26.5 %copy-start.4 = (s32[512]{0:T(512)S(1)}, s32[512]{0:T(512)}, u32[]{:S(2)}) copy-start(s32[512]{0:T(512)} %param.5) | copy-start | bytes 6148
  107.0 25.8 %all-to-all-start = ((f32[16,8,2176]{2,1,0:T(8,128)}), f32[16,8,2176]{2,1,0:T(8,128)S(1)}, u32[]{:S(2)}, u32[]{:S(2)}) async-start(f32[16,8,2176]{2,1,0:T(8,128)} %fusion.17), calls=%async_computation | async-start | bytes 2228224 | tf_op jit(solution)/shard_map/all_to_all | solution.py:243
  113.9 88.0 %all-gather.10.cloned.1.call-start = ((), (), s32[]{:S(2)}) async-start(), calls=%async_computation.8 | async-start | bytes 8982528 | tf_op jit(solution)/shard_map/all_gather | solution.py:296
  157.2 13.8 %all-to-all-start.1 = ((f32[16,16,256]{2,1,0:T(8,128)}), f32[16,16,256]{2,1,0:T(8,128)S(1)}, u32[]{:S(2)}, u32[]{:S(2)}) async-start(f32[16,16,256]{2,1,0:T(8,128)} %bitcast.4), calls=%async_computation.1 | async-start | bytes 524288 | tf_op jit(solution)/shard_map/all_to_all | solution.py:243
  171.7 12.5 %all-to-all-start.2 = ((f32[16,16,256]{2,1,0:T(8,128)}), f32[16,16,256]{2,1,0:T(8,128)S(1)}, u32[]{:S(2)}, u32[]{:S(2)}) async-start(f32[16,16,256]{2,1,0:T(8,128)} %broadcast_in_dim.37), calls=%async_computation.2 | async-start | bytes 524288 | tf_op jit(solution)/shard_map/all_to_all | solution.py:292
  192.8 0.7 copy-start
  201.9 113.7 %collective-permute-start = (bf16[512,2048]{1,0:T(8,128)(2,1)}, bf16[512,2048]{1,0:T(8,128)(2,1)}, u32[]{:S(2)}, u32[]{:S(2)}) collective-permute-start(bf16[512,2048]{1,0:T(8,128)(2,1)} %all-gather.8.cloned.1.call-done), channel_id=1, source_target_pairs={{0,64},{8,72},{16,80},{24,88},{32,96},{40,104},{48,112},{56,120},{... | collective-permute-start | bytes 6291464 | tf_op jit(solution)/shard_map/ppermute | solution.py:19
  203.4 112.2 %copy-start.3 = (s32[512]{0:T(512)S(1)}, s32[512]{0:T(512)}, u32[]{:S(2)}) copy-start(s32[512]{0:T(512)} %broadcast_subtract_fusion) | copy-start | bytes 6148
  315.7 3.1 copy-start.1
  318.7 4.9 %copy-start.5 = (bf16[2,2048,256]{2,1,0:T(8,128)(2,1)S(1)}, bf16[2,2048,256]{2,1,0:T(8,128)(2,1)}, u32[]{:S(2)}) copy-start(bf16[2,2048,256]{2,1,0:T(8,128)(2,1)} %get-tuple-element.20) | copy-start | bytes 6291460
  321.6 5.2 %collective-permute-start.1 = (f32[512]{0:T(512)S(1)}, f32[512]{0:T(512)S(1)}, u32[]{:S(2)}, u32[]{:S(2)}) collective-permute-start(f32[512]{0:T(512)S(1)} %get-tuple-element.22), channel_id=1, source_target_pairs={{0,64},{8,72},{16,80},{24,88},{32,96},{40,104},{48,112},{56,120},{... | collective-permute-start | bytes 6152 | tf_op jit(solution)/shard_map/ppermute | solution.py:19
  353.4 19.1 %all-to-all-start.4 = ((bf16[16,128,256]{2,1,0:T(8,128)(2,1)}), bf16[16,128,256]{2,1,0:T(8,128)(2,1)S(1)}, u32[]{:S(2)}, u32[]{:S(2)}) async-start(bf16[16,128,256]{2,1,0:T(8,128)(2,1)} %broadcast_in_dim.41), calls=%async_computation.4 | async-start | bytes 2097152 | tf_op jit(solution)/shard_map/all_to_all | solution.py:339
Sparse Core Ops, SparseCore 0:
  9.5 54.6 all-gather.5
  74.2 27.1 all-gather.7
  133.6 68.2 all-gather.9

commit v6 on v5

--- a/solution.py
+++ b/solution.py
@@ -3,6 +3,7 @@
 import jax
 import jax.numpy as jnp
 from jax import lax
+from jax.experimental.layout import Layout, with_layout_constraint
 from jax.experimental import pallas as pl
 from jax.experimental.pallas import tpu as pltpu
 from jax.sharding import PartitionSpec as P
@@ -272,7 +273,9 @@
     weight = lax.all_gather(proj_weight, "dp", axis=0, tiled=True)
     feature_sum = jnp.sum(features.astype(f32), axis=0)
     feature_sum = jnp.sum(lax.all_gather(feature_sum, "dp"), axis=0)
-    col_mean = jnp.sum(mat(three_parts(feature_sum), weight), axis=0) / batch_size
+    turned = with_layout_constraint(features.T, Layout(major_to_minor=(0, 1)))
+    sum_parts, turned = lax.optimization_barrier((three_parts(feature_sum), turned))
+    col_mean = jnp.sum(mat(sum_parts, weight), axis=0) / batch_size
     own_centered = (mat(features, weight) - col_mean).astype(bf16)
     centered = lax.all_gather(own_centered, "feat", axis=1, tiled=True)
 
@@ -343,7 +346,7 @@
     sum_moment = jnp.sum(sum_white[:, None] * moment.astype(f32), axis=0)
     back_mean = (own_total - sum_moment) / batch_size
     back_proj = (back_center - back_mean).astype(bf16)
-    grad = mat(features.T, back_proj).astype(bf16)
+    grad = mat(turned, back_proj).astype(bf16)
     return sum_shares(grad.reshape(dp_count, -1, own_cols), "dp")
 
 

time: 453 us -> 450 us (level)
  waiting for transfers between devices: 110 us -> 97.5 us
  local copies, waits for them, and re-layouts: 6.7 us -> 15 us
    all_gather x1, waiting for transfers between devices: 26.1 us -> 13.7 us  [body(): weight = lax.all_gather(proj_weight, 'dp', axis=0, tiled=True)]
    unnamed x12 -> x13, local copies, waits for them, and re-layouts: 1.11 us -> 13 us
  transfers between devices with their start and end apart: 9 -> 9, of which waited for: 8 -> 8; matrix products, arithmetic and copies ran while one was open for 4% -> 6% of each run, Pallas kernels for 27% -> 27%
where the time goes in v6:
time: 450 us; the launch traced here: 442 us
  Pallas kernels  121 us (27%)
  blocking collectives  120 us (27%)
  waiting for transfers between devices  97.5 us (22%)
  matrix products  33.1 us (7%)
  starting transfers between devices  23.1 us (5%)
  other arithmetic  19.8 us (4%)
  local copies, waits for them, and re-layouts  15 us (3%)
  between operations  13.6 us (3%)
    pallas_call x1, Pallas kernels, apply_inverse(): pl.pallas_call(lambda *refs: inverse_kernel(batch_size, *refs), out_shape...  112 us
    all_to_all x2, blocking collectives, sum_shares(): lax.all_to_all(array, axis, 0, 0, tiled=True).astype(f32)  73.2 us
    dot_general x10, matrix products, mat(): return jnp.dot(left, right, preferred_element_type=f32)  33.1 us
    all_gather x1, waiting for transfers between devices, body(): centered = lax.all_gather(own_centered, 'feat', axis=1, tiled=True)  27.1 us
    all_to_all x2, waiting for transfers between devices, sum_shares(): lax.all_to_all(array, axis, 0, 0, tiled=True).astype(f32)  25.4 us
    all_gather x1, blocking collectives, body(): feature_sum = jnp.sum(lax.all_gather(feature_sum, 'dp'), axis=0)  25.3 us
    all_gather x1, blocking collectives, body(): center_sum = jnp.sum(lax.all_gather(center_sum, 'dp'), axis=0)  21.1 us
    all_to_all x1, waiting for transfers between devices, body(): lax.all_to_all(jnp.broadcast_to(moment_share, (dp_count,) + moment_share....  14.5 us
  transfers between devices with their start and end apart: 9, of which 8 were waited for; matrix products, arithmetic and copies ran while one was open for 6% of the time, Pallas kernels for 27%

profile of v6, /device:TPU:0, one launch (start us, length us, event | category | flops | bytes accessed | tf_op | source)
XLA Modules:
  0.0 442.4 jit_solution(14833786490579499504)
XLA Ops:
  6.5 0.0 all-gather.6.cloned.1.call-start
  6.5 0.7 all-gather.6.cloned.1.call-update
  7.3 0.0 all-gather.8.cloned.1.call-start
  7.3 11.8 %copy.6 = bf16[512,8192]{0,1:T(8,128)(2,1)} copy(bf16[512,8192]{1,0:T(8,128)(2,1)} %param.3) | data formatting | bytes 16777216 | tf_op args[0]
  19.1 5.6 %convert_reduce_fusion = f32[8192]{0:T(1024)S(1)} fusion(bf16[512,8192]{1,0:T(8,128)(2,1)} %param.3), kind=kLoop, calls=%fused_computation | loop fusion | flops 8380416 | bytes 8421376 | tf_op jit(solution)/shard_map/reduce_sum | solution.py:274
  24.8 25.3 %all-gather = f32[131072]{0:T(1024)S(1)} all-gather(f32[8192]{0:T(1024)S(1)} %convert_reduce_fusion), channel_id=2, replica_groups=mesh['dp'=16,'feat'=8] {'dp'}, dimensions={0}, use_global_device_ids=true | all-gather | bytes 557056 | tf_op jit(solution)/shard_map/all_gather | solution.py:275
  50.1 0.1 reshape.133
  50.2 0.1 reduce_sum.144
  50.3 0.1 reduce-precision_convert_fusion.1
  50.4 0.1 fusion.31
  50.5 13.7 %all-gather.6.cloned.1.call-done = bf16[8192,256]{1,0:T(8,128)(2,1)} async-done(((bf16[512,256]{1,0:T(8,128)(2,1)}), bf16[8192,256]{1,0:T(8,128)(2,1)}) %all-gather.6.cloned.1.call-update) | async-done | bytes 4194320 | tf_op jit(solution)/shard_map/all_gather | solution.py:273
  64.2 3.0 convolution_reduce_fusion
  67.2 0.4 copy-done.2
  67.6 6.4 %fusion.11 = bf16[512,256]{1,0:T(8,128)(2,1)} fusion(bf16[512,8192]{1,0:T(8,128)(2,1)} %param.3, bf16[8192,256]{1,0:T(8,128)(2,1)S(1)} %copy-done.2, f32[256]{0:T(256)S(1)} %broadcast_multiply_fusion), kind=kOutput, calls=%fused_computation.24 | convolution fusion | flops 2147745792 | bytes 12846080 | tf_op jit(solution)/shard_map/dot_general | solution.py:29
  74.0 0.0 all-gather.8.cloned.1.call-update
  74.1 27.1 %all-gather.8.cloned.1.call-done = bf16[512,2048]{1,0:T(8,128)(2,1)} async-done(((bf16[512,256]{1,0:T(8,128)(2,1)}), bf16[512,2048]{1,0:T(8,128)(2,1)}) %all-gather.8.cloned.1.call-update) | async-done | bytes 2097168 | tf_op jit(solution)/shard_map/all_gather | solution.py:280
  101.2 2.1 fusion.39
  103.3 2.2 fusion.41
  105.5 1.3 fusion.19
  106.7 6.9 %all-to-all-start = ((f32[16,8,2176]{2,1,0:T(8,128)}), f32[16,8,2176]{2,1,0:T(8,128)S(1)}, u32[]{:S(2)}, u32[]{:S(2)}) async-start(f32[16,8,2176]{2,1,0:T(8,128)} %fusion.19), calls=%async_computation | async-start | bytes 2228224 | tf_op jit(solution)/shard_map/all_to_all | solution.py:244
  113.7 0.0 all-gather.10.cloned.1.call-start
  113.7 2.0 fusion.32
  115.8 16.8 %all-to-all-done = f32[16,8,2176]{2,1,0:T(8,128)S(1)} async-done(((f32[16,8,2176]{2,1,0:T(8,128)}), f32[16,8,2176]{2,1,0:T(8,128)S(1)}, u32[]{:S(2)}, u32[]{:S(2)}) %all-to-all-start) | async-done | bytes 1114144 | tf_op jit(solution)/shard_map/all_to_all | solution.py:244
  132.5 0.7 reduce_sum.147
  133.2 0.0 all-gather.10.cloned.1.call-update
  133.3 0.0 copy-done.4
  133.3 0.6 broadcast_subtract_fusion
  133.9 2.0 convert_reduce_fusion.2
  135.8 21.1 %all-gather.1 = f32[32768]{0:T(1024)S(1)} all-gather(f32[2048]{0:T(1024)S(1)} %convert_reduce_fusion.2), channel_id=3, replica_groups=mesh['dp'=16,'feat'=8] {'dp'}, dimensions={0}, use_global_device_ids=true | all-gather | bytes 139264 | tf_op jit(solution)/shard_map/all_gather | solution.py:303
  156.9 5.1 %all-to-all-start.1 = ((f32[16,16,256]{2,1,0:T(8,128)}), f32[16,16,256]{2,1,0:T(8,128)S(1)}, u32[]{:S(2)}, u32[]{:S(2)}) async-start(f32[16,16,256]{2,1,0:T(8,128)} %bitcast.5), calls=%async_computation.1 | async-start | bytes 524288 | tf_op jit(solution)/shard_map/all_to_all | solution.py:244
  162.1 8.6 %all-to-all-done.1 = f32[16,16,256]{2,1,0:T(8,128)S(1)} async-done(((f32[16,16,256]{2,1,0:T(8,128)}), f32[16,16,256]{2,1,0:T(8,128)S(1)}, u32[]{:S(2)}, u32[]{:S(2)}) %all-to-all-start.1) | async-done | bytes 262176 | tf_op jit(solution)/shard_map/all_to_all | solution.py:244
  170.7 0.7 broadcast_in_dim.37
  171.5 3.7 all-to-all-start.2
  175.2 3.3 pad_maximum_fusion.refs_3_
  178.5 5.4 %all-to-all-done.2 = f32[16,16,256]{2,1,0:T(8,128)S(1)} async-done(((f32[16,16,256]{2,1,0:T(8,128)}), f32[16,16,256]{2,1,0:T(8,128)S(1)}, u32[]{:S(2)}, u32[]{:S(2)}) %all-to-all-start.2) | async-done | bytes 262176 | tf_op jit(solution)/shard_map/all_to_all | solution.py:295
  183.9 8.6 %shard_map.37.refs_2_ = f32[256,256]{1,0:T(8,128)S(1)} custom-call(f32[256,256]{1,0:T(8,128)S(1)} %bitcast.36), custom_call_target="tpu_custom_call" | custom-call | tf_op jit(solution)/shard_map/pallas_call | solution.py:104
  192.5 0.0 copy-start
  192.5 0.7 copy-done
  193.2 8.4 %all-gather.10.cloned.1.call-done = f32[1024,2176]{1,0:T(8,128)} async-done(((f32[8,2176]{1,0:T(8,128)}), f32[1024,2176]{1,0:T(8,128)}) %all-gather.10.cloned.1.call-update) | async-done | bytes 8912912 | tf_op jit(solution)/shard_map/all_gather | solution.py:299
  201.6 1.6 collective-permute-start
  203.2 112.2 %shard_map.38 = (f32[528,2048]{1,0:T(8,128)}, bf16[2,2048,256]{2,1,0:T(8,128)(2,1)}) custom-call(s32[1]{0:T(128)} %bitcast.2.refs_0_, f32[8,128,2176]{2,1,0:T(8,128)} %bitcast.47, f32[256,256]{1,0:T(8,128)} %copy-done, bf16[528,2048]{1,0:T(8,128)(2,1)} %pad_maximum_fusion.refs_3_), custom_call_target="tpu_custom_call" | custom-call | flops 149999992832 | bytes 20000000 | tf_op jit(solution)/shard_map/pallas_call | solution.py:220
  315.3 0.0 collective-permute-done
  315.3 0.0 copy-done.3
  315.3 3.0 convolution_convert_fusion.1
  318.4 0.0 copy-done.1
  318.4 0.0 copy-start.5
  318.4 2.8 multiply_reduce_fusion
  321.2 2.0 collective-permute-start.1
  323.2 0.7 fusion.22
  323.9 2.4 collective-permute-done.1
  326.4 0.2 select_reduce_fusion
  326.7 0.7 fusion.59
  327.4 2.4 fusion
  329.8 0.1 pad_maximum_fusion.1
  329.9 21.9 %all_to_all.30 = bf16[16,144,256]{2,1,0:T(8,128)(2,1)S(1)} all-to-all(bf16[16,144,256]{2,1,0:T(8,128)(2,1)S(1)} %pad_maximum_fusion.1), channel_id=1, replica_groups=mesh['dp'=16,'feat'=8] {'dp'}, dimensions={0} | all-to-all | bytes 2359296 | tf_op jit(solution)/shard_map/all_to_all | solution.py:244
  351.8 0.2 convert_reduce_fusion.3
  352.0 1.1 broadcast_in_dim.41
  353.0 3.7 all-to-all-start.4
  356.7 0.9 slice_reduce_fusion
  357.6 14.5 %all-to-all-done.4 = bf16[16,128,256]{2,1,0:T(8,128)(2,1)S(1)} async-done(((bf16[16,128,256]{2,1,0:T(8,128)(2,1)}), bf16[16,128,256]{2,1,0:T(8,128)(2,1)S(1)}, u32[]{:S(2)}, u32[]{:S(2)}) %all-to-all-start.4) | async-done | bytes 1048608 | tf_op jit(solution)/shard_map/all_to_all | solution.py:342
  372.1 0.3 multiply_reduce_fusion.2
  372.5 10.5 %convolution_convert_fusion = bf16[8192,256]{1,0:T(8,128)(2,1)} fusion(bf16[8192,512]{1,0:T(8,128)(2,1)} %bitcast.37, f32[512,256]{1,0:T(8,128)S(1)} %get-tuple-element.39, bf16[2048,256]{1,0:T(8,128)(2,1)S(1)} %bitcast.39, f32[256]{0:T(256)S(1)} %bitcast.44, f32[528,2048]{1,0:T(8,128)} %get-tuple-element.22), kind=kOutput, calls=%fused_computation.1 | convolution fusion | flops 2686844928 | bytes 16253952 | tf_op jit(solution)/shard_map/dot_general | solution.py:29
  383.0 51.3 %all_to_all.31 = bf16[16,512,256]{2,1,0:T(8,128)(2,1)S(1)} all-to-all(bf16[16,512,256]{2,1,0:T(8,128)(2,1)} %bitcast.38), channel_id=1, replica_groups=mesh['dp'=16,'feat'=8] {'dp'}, dimensions={0} | all-to-all | bytes 8388608 | tf_op jit(solution)/shard_map/all_to_all | solution.py:244
  434.3 1.4 convert_reduce_fusion.1
  (18 shorter events, 0.2 us)
Async XLA Ops:
  6.5 57.6 %all-gather.6.cloned.1.call-start = ((), (), s32[]{:S(2)}) async-start(), calls=%async_computation.6 | async-start | bytes 4456448 | tf_op jit(solution)/shard_map/all_gather | solution.py:273
  7.3 93.9 %all-gather.8.cloned.1.call-start = ((), (), s32[]{:S(2)}) async-start(), calls=%async_computation.7 | async-start | bytes 2359296 | tf_op jit(solution)/shard_map/all_gather | solution.py:280
  64.2 3.4 copy-start.2
  106.7 26.5 %copy-start.4 = (s32[512]{0:T(512)S(1)}, s32[512]{0:T(512)}, u32[]{:S(2)}) copy-start(s32[512]{0:T(512)} %param.5) | copy-start | bytes 6148
  106.7 25.8 %all-to-all-start = ((f32[16,8,2176]{2,1,0:T(8,128)}), f32[16,8,2176]{2,1,0:T(8,128)S(1)}, u32[]{:S(2)}, u32[]{:S(2)}) async-start(f32[16,8,2176]{2,1,0:T(8,128)} %fusion.19), calls=%async_computation | async-start | bytes 2228224 | tf_op jit(solution)/shard_map/all_to_all | solution.py:244
  113.7 87.9 %all-gather.10.cloned.1.call-start = ((), (), s32[]{:S(2)}) async-start(), calls=%async_computation.8 | async-start | bytes 8982528 | tf_op jit(solution)/shard_map/all_gather | solution.py:299
  156.9 13.8 %all-to-all-start.1 = ((f32[16,16,256]{2,1,0:T(8,128)}), f32[16,16,256]{2,1,0:T(8,128)S(1)}, u32[]{:S(2)}, u32[]{:S(2)}) async-start(f32[16,16,256]{2,1,0:T(8,128)} %bitcast.5), calls=%async_computation.1 | async-start | bytes 524288 | tf_op jit(solution)/shard_map/all_to_all | solution.py:244
  171.5 12.4 %all-to-all-start.2 = ((f32[16,16,256]{2,1,0:T(8,128)}), f32[16,16,256]{2,1,0:T(8,128)S(1)}, u32[]{:S(2)}, u32[]{:S(2)}) async-start(f32[16,16,256]{2,1,0:T(8,128)} %broadcast_in_dim.37), calls=%async_computation.2 | async-start | bytes 524288 | tf_op jit(solution)/shard_map/all_to_all | solution.py:295
  192.5 0.7 copy-start
  201.6 113.8 %collective-permute-start = (bf16[512,2048]{1,0:T(8,128)(2,1)}, bf16[512,2048]{1,0:T(8,128)(2,1)}, u32[]{:S(2)}, u32[]{:S(2)}) collective-permute-start(bf16[512,2048]{1,0:T(8,128)(2,1)} %all-gather.8.cloned.1.call-done), channel_id=1, source_target_pairs={{0,64},{8,72},{16,80},{24,88},{32,96},{40,104},{48,112},{56,120},{... | collective-permute-start | bytes 6291464 | tf_op jit(solution)/shard_map/ppermute | solution.py:20
  203.2 112.2 %copy-start.3 = (s32[512]{0:T(512)S(1)}, s32[512]{0:T(512)}, u32[]{:S(2)}) copy-start(s32[512]{0:T(512)} %broadcast_subtract_fusion) | copy-start | bytes 6148
  315.3 3.0 copy-start.1
  318.4 4.8 %copy-start.5 = (bf16[2,2048,256]{2,1,0:T(8,128)(2,1)S(1)}, bf16[2,2048,256]{2,1,0:T(8,128)(2,1)}, u32[]{:S(2)}) copy-start(bf16[2,2048,256]{2,1,0:T(8,128)(2,1)} %get-tuple-element.24) | copy-start | bytes 6291460
  321.2 5.2 %collective-permute-start.1 = (f32[512]{0:T(512)S(1)}, f32[512]{0:T(512)S(1)}, u32[]{:S(2)}, u32[]{:S(2)}) collective-permute-start(f32[512]{0:T(512)S(1)} %get-tuple-element.26), channel_id=1, source_target_pairs={{0,64},{8,72},{16,80},{24,88},{32,96},{40,104},{48,112},{56,120},{... | collective-permute-start | bytes 6152 | tf_op jit(solution)/shard_map/ppermute | solution.py:20
  353.0 19.1 %all-to-all-start.4 = ((bf16[16,128,256]{2,1,0:T(8,128)(2,1)}), bf16[16,128,256]{2,1,0:T(8,128)(2,1)S(1)}, u32[]{:S(2)}, u32[]{:S(2)}) async-start(bf16[16,128,256]{2,1,0:T(8,128)(2,1)} %broadcast_in_dim.41), calls=%async_computation.4 | async-start | bytes 2097152 | tf_op jit(solution)/shard_map/all_to_all | solution.py:342
Sparse Core Ops, SparseCore 0:
  9.5 54.6 all-gather.5
  74.2 26.9 all-gather.7
  133.4 68.1 all-gather.9
